TPU v7x, 32 devices: a whole 2x2x4 slice. The times are simulated.
32 devices in a mesh: ctx: 8 (over y, x, core), fsdp: 4 (over z).
Axes of the slice: x: 2, y: 2, z: 4, core: 2. Of those that a mesh axis runs over, the one named last changes fastest.
Arguments:
- inputs: float32 [4, 1024, 1536], P('fsdp', 'ctx'), may hold values from -6 to 6
- teacher: float32 [4, 1024, 1536], P('fsdp', 'ctx'), may hold values from -6 to 6
- lengths: int32 [4], P('fsdp'), may hold values from 897 to 1024, as said below
- w_query: bfloat16 [1536, 1536], P('fsdp'), may hold values from -0.15625 to 0.15625
- w_key: bfloat16 [1536, 768], P('fsdp'), may hold values from -0.15625 to 0.15625
- w_value: bfloat16 [1536, 768], P('fsdp'), may hold values from -0.15625 to 0.15625
- w_out: bfloat16 [1536, 1536], P('fsdp'), may hold values from -1.25 to 1.25
- w_gate: bfloat16 [1536, 4096], P('fsdp'), may hold values from -0.15625 to 0.15625
- w_up: bfloat16 [1536, 4096], P('fsdp'), may hold values from -0.15625 to 0.15625
- w_down: bfloat16 [4096, 1536], P('fsdp'), may hold values from -0.09375 to 0.09375
- gain_attn: bfloat16 [1536], P('fsdp'), may hold values from 0.5 to 1.5
- gain_ffn: bfloat16 [1536], P('fsdp'), may hold values from 0.5 to 1.5
Outputs:
- output: float32 [4, 1024, 1536], P('fsdp', 'ctx')
- loss_value: float32 [], replicated
- grad_inputs: float32 [4, 1024, 1536], P('fsdp', 'ctx')
- grad_query: float32 [1536, 1536], P('fsdp')
- grad_key: float32 [1536, 768], P('fsdp')
- grad_value: float32 [1536, 768], P('fsdp')
- grad_out: float32 [1536, 1536], P('fsdp')
- grad_gate: float32 [1536, 4096], P('fsdp')
- grad_up: float32 [1536, 4096], P('fsdp')
- grad_down: float32 [4096, 1536], P('fsdp')
- grad_gain_attn: float32 [1536], P('fsdp')
- grad_gain_ffn: float32 [1536], P('fsdp')
Inputs may be any that keep to these rules, and one draw needn't show every extreme that they name: `lengths`: each sequence has more than 896 valid tokens, and some sequence fills all 1024.
All inputs are finite; a program needn't handle non-finite values.
Results may differ from a plain program's by a relative error of at most 0.023.
Values may be sent and summed in bfloat16 or wider, within the bound.
No kernel may reach another device: no remote copies, remote signals or barrier semaphores. Data moves between devices by JAX's collectives and lax.ppermute only.
A program may use at most 320 MiB of HBM per device.

v0:
```python
import jax
import jax.numpy as jnp
from jax import lax
from jax.sharding import PartitionSpec as P

HEADS = 16
KV_HEADS = 8
HEAD_DIM = 96


eps_norm = 1e-05
rope_base = 100000.0
masked_value = -1e30


def times_transposed(left, right):
    return lax.dot_general(
        left, right, (((1,), (1,)), ((), ())), preferred_element_type=jnp.float32
    )


def transposed_times(left, right):
    return lax.dot_general(
        left, right, (((0,), (0,)), ((), ())), preferred_element_type=jnp.float32
    )


def norm_scale(features):
    return lax.rsqrt(jnp.mean(features * features, axis=-1, keepdims=True) + eps_norm)


def norm_back(upstream, features, row_scale, gain_vector):
    weighted = upstream * gain_vector
    inner_mean = jnp.mean(weighted * features, axis=-1, keepdims=True)
    grad_rows = row_scale * weighted - features * (row_scale * row_scale * row_scale) * inner_mean
    return (grad_rows, jnp.sum(upstream * (features * row_scale), axis=0))


def rotate(features, positions, sign):
    half_dim = features.shape[-1] // 2
    frequencies = rope_base ** (
        -(jnp.arange(half_dim, dtype=jnp.float32) * 2.0) / features.shape[-1]
    )
    angles = positions.astype(jnp.float32)[:, None] * frequencies[None, :]
    angles = jnp.concatenate([angles, angles], axis=-1)[:, None, :]
    turned = jnp.concatenate([-features[..., half_dim:], features[..., :half_dim]], axis=-1)
    return features * jnp.cos(angles) + sign * turned * jnp.sin(angles)


def local(
    inputs,
    teacher,
    lengths,
    w_query,
    w_key,
    w_value,
    w_out,
    w_gate,
    w_up,
    w_down,
    gain_attn,
    gain_ffn,
):
    hidden_in = inputs[0]
    target = teacher[0]
    seq_length = lengths[0]
    token_count = hidden_in.shape[0]
    model_width = hidden_in.shape[1]
    group_size = HEADS // KV_HEADS
    kv_width = KV_HEADS * HEAD_DIM
    scale_attn = HEAD_DIM ** (-0.5)
    first_position = lax.axis_index("ctx") * token_count
    last_position = first_position + token_count - 1
    positions = first_position + jnp.arange(token_count, dtype=jnp.int32)
    query_all, key_all, value_all, out_all, gain_one = (
        lax.all_gather(w_query, "fsdp", axis=0, tiled=True),
        lax.all_gather(w_key, "fsdp", axis=0, tiled=True),
        lax.all_gather(w_value, "fsdp", axis=0, tiled=True),
        lax.all_gather(w_out, "fsdp", axis=0, tiled=True),
        lax.all_gather(gain_attn, "fsdp", axis=0, tiled=True),
    )
    scale_one = norm_scale(hidden_in)
    normed_one = (hidden_in * scale_one * gain_one.astype(jnp.float32)).astype(jnp.bfloat16)
    query_lin = jnp.dot(normed_one, query_all, preferred_element_type=jnp.float32)
    key_lin = jnp.dot(normed_one, key_all, preferred_element_type=jnp.float32)
    value_row_block = jnp.dot(normed_one, value_all, preferred_element_type=jnp.float32).astype(
        jnp.bfloat16
    )
    queries = rotate(query_lin.reshape(token_count, HEADS, HEAD_DIM), positions, 1.0).astype(
        jnp.bfloat16
    )
    key_row_block = (
        rotate(key_lin.reshape(token_count, KV_HEADS, HEAD_DIM), positions, 1.0)
        .astype(jnp.bfloat16)
        .reshape(token_count, kv_width)
    )
    grouped_rows = queries.reshape(token_count, KV_HEADS, group_size, HEAD_DIM)

    def block_scores(key_block, block_start):
        head_key_rows = key_block.reshape(key_block.shape[0], KV_HEADS, HEAD_DIM)
        logit_scores = (
            jnp.einsum(
                "oqkj,lqj->qkol", grouped_rows, head_key_rows, preferred_element_type=jnp.float32
            )
            * scale_attn
        )
        key_positions = block_start + jnp.arange(key_block.shape[0], dtype=jnp.int32)
        allowed = (key_positions[None, :] <= positions[:, None]) & (
            key_positions[None, :] < seq_length
        )
        return (logit_scores, allowed, head_key_rows)

    start_state = (
        jnp.full((KV_HEADS, group_size, token_count), masked_value, jnp.float32),
        jnp.zeros((KV_HEADS, group_size, token_count), jnp.float32),
        jnp.zeros((KV_HEADS, group_size, token_count, HEAD_DIM), jnp.float32),
    )
    key_piece = lax.all_gather(key_row_block, "ctx", axis=0, tiled=True)
    value_piece = lax.all_gather(value_row_block, "ctx", axis=0, tiled=True)
    piece_rows = key_piece.shape[0]
    fold_block_rows = 512

    def fold_step(fold_state, block_index):
        key_start = block_index * fold_block_rows

        def fold_compute(state_in):
            running_max, running_sum, running_out = state_in
            key_block = lax.dynamic_slice_in_dim(
                key_piece, block_index * fold_block_rows, fold_block_rows, 0
            )
            value_block = lax.dynamic_slice_in_dim(
                value_piece, block_index * fold_block_rows, fold_block_rows, 0
            )
            head_value_rows = value_block.reshape(fold_block_rows, KV_HEADS, HEAD_DIM)
            logit_scores, allowed, head_key_rows = block_scores(key_block, key_start)
            new_max = jnp.maximum(
                running_max, jnp.max(jnp.where(allowed, logit_scores, masked_value), axis=-1)
            )
            weights_block = jnp.where(allowed, jnp.exp(logit_scores - new_max[..., None]), 0.0)
            factor = jnp.exp(running_max - new_max)
            new_sum = running_sum * factor + jnp.sum(weights_block, axis=-1)
            new_out = running_out * factor[..., None] + jnp.einsum(
                "couk,kcz->couz",
                weights_block.astype(jnp.bfloat16),
                head_value_rows,
                preferred_element_type=jnp.float32,
            )
            return (new_max, new_sum, new_out)

        def fold_passed(state_in):
            return state_in

        return (lax.cond(key_start <= last_position, fold_compute, fold_passed, fold_state), None)

    fold_state, unused = lax.scan(fold_step, start_state, jnp.arange(piece_rows // fold_block_rows))
    running_max, running_sum, running_out = fold_state
    log_total = running_max + jnp.log(running_sum)
    attended_head_rows = (running_out / running_sum[..., None]).transpose(2, 0, 1, 3)
    attended = attended_head_rows.reshape(token_count, model_width)
    attended_low = attended.astype(jnp.bfloat16)
    middle = hidden_in + jnp.dot(attended_low, out_all, preferred_element_type=jnp.float32)
    gate_all, up_all, down_all, gain_two = (
        lax.all_gather(w_gate, "fsdp", axis=0, tiled=True),
        lax.all_gather(w_up, "fsdp", axis=0, tiled=True),
        lax.all_gather(w_down, "fsdp", axis=0, tiled=True),
        lax.all_gather(gain_ffn, "fsdp", axis=0, tiled=True),
    )
    scale_two = norm_scale(middle)
    normed_two = (middle * scale_two * gain_two.astype(jnp.float32)).astype(jnp.bfloat16)
    gate_pre = jnp.dot(normed_two, gate_all, preferred_element_type=jnp.float32)
    up_value = jnp.dot(normed_two, up_all, preferred_element_type=jnp.float32)
    activated = (jax.nn.silu(gate_pre) * up_value).astype(jnp.bfloat16)
    output = middle + jnp.dot(activated, down_all, preferred_element_type=jnp.float32)
    valid_rows = (positions < seq_length).astype(jnp.float32)
    residual_error = output - target
    squares = jnp.sum(valid_rows[:, None] * residual_error * residual_error)
    total_squares, valid_count = lax.psum((squares, jnp.sum(valid_rows)), ("ctx", "fsdp"))
    loss_value = total_squares / valid_count
    gate_all, up_all, down_all = (
        lax.all_gather(w_gate, "fsdp", axis=0, tiled=True),
        lax.all_gather(w_up, "fsdp", axis=0, tiled=True),
        lax.all_gather(w_down, "fsdp", axis=0, tiled=True),
    )
    grad_output = valid_rows[:, None] * (2.0 * residual_error) / valid_count
    grad_low = grad_output.astype(jnp.bfloat16)
    grad_down_full = transposed_times(activated, grad_low)
    grad_act = times_transposed(grad_low, down_all)
    sigmoid_gate = jax.nn.sigmoid(gate_pre)
    grad_gate_pre = (
        grad_act * up_value * (sigmoid_gate * (1.0 + gate_pre * (1.0 - sigmoid_gate)))
    ).astype(jnp.bfloat16)
    grad_up_value = (grad_act * jax.nn.silu(gate_pre)).astype(jnp.bfloat16)
    grad_gate_full = transposed_times(normed_two, grad_gate_pre)
    grad_up_full = transposed_times(normed_two, grad_up_value)
    grad_normed_two = times_transposed(grad_gate_pre, gate_all) + times_transposed(
        grad_up_value, up_all
    )
    back_two, grad_gain_two = norm_back(
        grad_normed_two, middle, scale_two, gain_two.astype(jnp.float32)
    )
    grad_middle = grad_output + back_two
    shard_gate, shard_up, shard_down, shard_gain_two = (
        lax.psum_scatter(
            grad_gate_full.astype(jnp.bfloat16), "fsdp", scatter_dimension=0, tiled=True
        ).astype(jnp.float32),
        lax.psum_scatter(
            grad_up_full.astype(jnp.bfloat16), "fsdp", scatter_dimension=0, tiled=True
        ).astype(jnp.float32),
        lax.psum_scatter(
            grad_down_full.astype(jnp.bfloat16), "fsdp", scatter_dimension=0, tiled=True
        ).astype(jnp.float32),
        lax.psum_scatter(
            grad_gain_two.astype(jnp.bfloat16), "fsdp", scatter_dimension=0, tiled=True
        ).astype(jnp.float32),
    )
    query_all, key_all, value_all, out_all = (
        lax.all_gather(w_query, "fsdp", axis=0, tiled=True),
        lax.all_gather(w_key, "fsdp", axis=0, tiled=True),
        lax.all_gather(w_value, "fsdp", axis=0, tiled=True),
        lax.all_gather(w_out, "fsdp", axis=0, tiled=True),
    )
    grad_branch = grad_middle.astype(jnp.bfloat16)
    grad_out_full = transposed_times(attended_low, grad_branch)
    grad_attended = times_transposed(grad_branch, out_all).astype(jnp.bfloat16)
    head_gradient_rows = grad_attended.reshape(token_count, KV_HEADS, group_size, HEAD_DIM)
    row_difference = jnp.einsum(
        "fyuo,fyuo->yuf", head_gradient_rows.astype(jnp.float32), attended_head_rows
    )
    keys_all, values_all = (
        lax.all_gather(key_row_block, "ctx", axis=0, tiled=True),
        lax.all_gather(value_row_block, "ctx", axis=0, tiled=True),
    )
    seq_rows = keys_all.shape[0]
    block_rows = min(512, seq_rows)

    def back_step(query_acc, block_index):
        key_start = block_index * block_rows

        def back_compute(acc_in):
            key_block = lax.dynamic_slice_in_dim(keys_all, key_start, block_rows, 0)
            value_block = lax.dynamic_slice_in_dim(values_all, key_start, block_rows, 0)
            head_value_rows = value_block.reshape(block_rows, KV_HEADS, HEAD_DIM)
            logit_scores, allowed, head_key_rows = block_scores(key_block, key_start)
            probs_full = jnp.where(allowed, jnp.exp(logit_scores - log_total[..., None]), 0.0)
            grad_probs = jnp.einsum(
                "oqkj,lqj->qkol",
                head_gradient_rows,
                head_value_rows,
                preferred_element_type=jnp.float32,
            )
            score_gradients = (probs_full * (grad_probs - row_difference[..., None])).astype(
                jnp.bfloat16
            )
            value_terms = jnp.einsum(
                "weaz,awex->zwx",
                probs_full.astype(jnp.bfloat16),
                head_gradient_rows,
                preferred_element_type=jnp.float32,
            )
            key_terms = (
                jnp.einsum(
                    "weaz,awex->zwx",
                    score_gradients,
                    grouped_rows,
                    preferred_element_type=jnp.float32,
                )
                * scale_attn
            )
            acc_out = (
                acc_in
                + jnp.einsum(
                    "lqpc,cli->plqi",
                    score_gradients,
                    head_key_rows,
                    preferred_element_type=jnp.float32,
                )
                * scale_attn
            )
            return (
                acc_out,
                key_terms.reshape(block_rows, kv_width),
                value_terms.reshape(block_rows, kv_width),
            )

        def back_passed(acc_in):
            empty_terms = jnp.zeros((block_rows, kv_width), jnp.float32)
            return (acc_in, empty_terms, empty_terms)

        acc_out, key_terms, value_terms = lax.cond(
            key_start <= last_position, back_compute, back_passed, query_acc
        )
        return (acc_out, (key_terms, value_terms))

    query_start = jnp.zeros((token_count, KV_HEADS, group_size, HEAD_DIM), jnp.float32)
    grad_rotated, (key_parts, value_parts) = lax.scan(
        back_step, query_start, jnp.arange(seq_rows // block_rows)
    )
    grad_keys_rot, grad_values = (
        lax.psum_scatter(
            key_parts.reshape(seq_rows, kv_width).astype(jnp.bfloat16),
            "ctx",
            scatter_dimension=0,
            tiled=True,
        ).astype(jnp.float32),
        lax.psum_scatter(
            value_parts.reshape(seq_rows, kv_width).astype(jnp.bfloat16),
            "ctx",
            scatter_dimension=0,
            tiled=True,
        ).astype(jnp.float32),
    )
    grad_query_lin = (
        rotate(grad_rotated.reshape(token_count, HEADS, HEAD_DIM), positions, -1.0)
        .reshape(token_count, model_width)
        .astype(jnp.bfloat16)
    )
    grad_key_lin = (
        rotate(grad_keys_rot.reshape(token_count, KV_HEADS, HEAD_DIM), positions, -1.0)
        .reshape(token_count, kv_width)
        .astype(jnp.bfloat16)
    )
    grad_value_low = grad_values.astype(jnp.bfloat16)
    grad_query_full = transposed_times(normed_one, grad_query_lin)
    grad_key_full = transposed_times(normed_one, grad_key_lin)
    grad_value_full = transposed_times(normed_one, grad_value_low)
    grad_normed_one = (
        times_transposed(grad_query_lin, query_all)
        + times_transposed(grad_key_lin, key_all)
        + times_transposed(grad_value_low, value_all)
    )
    back_one, grad_gain_one = norm_back(
        grad_normed_one, hidden_in, scale_one, gain_one.astype(jnp.float32)
    )
    grad_hidden = grad_middle + back_one
    shard_query, shard_key, shard_value, shard_out, shard_gain_one = (
        lax.psum_scatter(
            grad_query_full.astype(jnp.bfloat16), "fsdp", scatter_dimension=0, tiled=True
        ).astype(jnp.float32),
        lax.psum_scatter(
            grad_key_full.astype(jnp.bfloat16), "fsdp", scatter_dimension=0, tiled=True
        ).astype(jnp.float32),
        lax.psum_scatter(
            grad_value_full.astype(jnp.bfloat16), "fsdp", scatter_dimension=0, tiled=True
        ).astype(jnp.float32),
        lax.psum_scatter(
            grad_out_full.astype(jnp.bfloat16), "fsdp", scatter_dimension=0, tiled=True
        ).astype(jnp.float32),
        lax.psum_scatter(
            grad_gain_one.astype(jnp.bfloat16), "fsdp", scatter_dimension=0, tiled=True
        ).astype(jnp.float32),
    )
    (
        final_query,
        final_key,
        final_value,
        final_out,
        final_gate,
        final_up,
        final_down,
        final_gain_one,
        final_gain_two,
    ) = (
        lax.psum(shard_query.astype(jnp.bfloat16), "ctx").astype(jnp.float32),
        lax.psum(shard_key.astype(jnp.bfloat16), "ctx").astype(jnp.float32),
        lax.psum(shard_value.astype(jnp.bfloat16), "ctx").astype(jnp.float32),
        lax.psum(shard_out.astype(jnp.bfloat16), "ctx").astype(jnp.float32),
        lax.psum(shard_gate.astype(jnp.bfloat16), "ctx").astype(jnp.float32),
        lax.psum(shard_up.astype(jnp.bfloat16), "ctx").astype(jnp.float32),
        lax.psum(shard_down.astype(jnp.bfloat16), "ctx").astype(jnp.float32),
        lax.psum(shard_gain_one.astype(jnp.bfloat16), "ctx").astype(jnp.float32),
        lax.psum(shard_gain_two.astype(jnp.bfloat16), "ctx").astype(jnp.float32),
    )
    return (
        output[None],
        loss_value,
        grad_hidden[None],
        final_query,
        final_key,
        final_value,
        final_out,
        final_gate,
        final_up,
        final_down,
        final_gain_one,
        final_gain_two,
    )


def solution(mesh):
    return jax.shard_map(
        local,
        mesh=mesh,
        in_specs=(
            P("fsdp", "ctx", None),
            P("fsdp", "ctx", None),
            P("fsdp"),
            P("fsdp", None),
            P("fsdp", None),
            P("fsdp", None),
            P("fsdp", None),
            P("fsdp", None),
            P("fsdp", None),
            P("fsdp", None),
            P("fsdp"),
            P("fsdp"),
        ),
        out_specs=(
            P("fsdp", "ctx", None),
            P(),
            P("fsdp", "ctx", None),
            P("fsdp", None),
            P("fsdp", None),
            P("fsdp", None),
            P("fsdp", None),
            P("fsdp", None),
            P("fsdp", None),
            P("fsdp", None),
            P("fsdp"),
            P("fsdp"),
        ),
        check_vma=False,
    )
```

profile of v0, /device:TPU:0, one launch (start us, length us, event | category | flops | bytes accessed | tf_op | source)
XLA Modules:
  0.0 2326.5 jit_solution(1958824486703246302)
XLA Ops:
  9.4 13.5 all-gather
  26.1 36.7 %all-gather.18.cloned.1.call-done = bf16[1536,768]{1,0:T(8,128)(2,1)} async-done(((bf16[384,768]{1,0:T(8,128)(2,1)}), bf16[1536,768]{1,0:T(8,128)(2,1)}) %all-gather.18.cloned.1.call-update) | async-done | bytes 2359312 | tf_op jit(solution)/shard_map/all_gather | solution.py:78
  67.4 46.3 %all-gather.12.cloned.1.call-done = bf16[1536,768]{1,0:T(8,128)(2,1)} async-done(((bf16[384,768]{1,0:T(8,128)(2,1)}), bf16[1536,768]{1,0:T(8,128)(2,1)}) %all-gather.12.cloned.1.call-update) | async-done | bytes 2359312 | tf_op jit(solution)/shard_map/all_gather | solution.py:77
  122.5 12.4 all-gather.1
  143.3 88.3 %all-gather.16.cloned.1.call-done = bf16[1536,1536]{1,0:T(8,128)(2,1)} async-done(((bf16[384,1536]{1,0:T(8,128)(2,1)}), bf16[1536,1536]{1,0:T(8,128)(2,1)}) %all-gather.16.cloned.1.call-update) | async-done | bytes 4718608 | tf_op jit(solution)/shard_map/all_gather | solution.py:76
  242.3 15.9 all-gather.14.cloned.1.call-done
  258.3 8.5 while.33
  266.9 82.2 %all-gather.22.cloned.1.call-done = bf16[1536,1536]{1,0:T(8,128)(2,1)} async-done(((bf16[384,1536]{1,0:T(8,128)(2,1)}), bf16[1536,1536]{1,0:T(8,128)(2,1)}) %all-gather.22.cloned.1.call-update) | async-done | bytes 4718608 | tf_op jit(solution)/shard_map/all_gather | solution.py:79
  353.1 214.2 %all-gather.24.cloned.1.call-done = bf16[1536,4096]{1,0:T(8,128)(2,1)} async-done(((bf16[384,4096]{1,0:T(8,128)(2,1)}), bf16[1536,4096]{1,0:T(8,128)(2,1)}) %all-gather.24.cloned.1.call-update) | async-done | bytes 12582928 | tf_op jit(solution)/shard_map/all_gather | solution.py:163
  567.4 7.7 fusion.64
  575.1 210.3 %all-gather.26.cloned.1.call-done = bf16[1536,4096]{1,0:T(8,128)(2,1)} async-done(((bf16[384,4096]{1,0:T(8,128)(2,1)}), bf16[1536,4096]{1,0:T(8,128)(2,1)}) %all-gather.26.cloned.1.call-update) | async-done | bytes 12582928 | tf_op jit(solution)/shard_map/all_gather | solution.py:164
  785.4 8.6 multiply_convert_fusion.2
  794.0 209.4 %all-gather.28.cloned.1.call-done = bf16[4096,1536]{1,0:T(8,128)(2,1)} async-done(((bf16[1024,1536]{1,0:T(8,128)(2,1)}), bf16[4096,1536]{1,0:T(8,128)(2,1)}) %all-gather.28.cloned.1.call-update) | async-done | bytes 12582928 | tf_op jit(solution)/shard_map/all_gather | solution.py:165
  1003.4 8.1 fusion.36
  1011.5 38.8 %all-reduce.2 = (f32[]{:T(128)}, f32[]{:T(128)}) all-reduce(f32[]{:T(128)} %get-tuple-element.496, f32[]{:T(128)} %get-tuple-element.463), channel_id=1, replica_groups=mesh['ctx'=8,'fsdp'=4] {'ctx','fsdp'}, use_global_device_ids=true, to_apply=%region_9.10 | all-reduce | flops 2 | bytes 16 | tf_op jit(solution)/shard_map/psum | solution.py:177
  1052.3 10.4 multiply_convert_fusion
  1062.7 9.6 fusion.65
  1072.3 9.1 multiply_reduce_fusion
  1086.4 16.2 while.34
  1087.9 9.7 conditional.7
  1104.4 46.3 %reduce-scatter.10.cloned.1.call-done = bf16[128,768]{1,0:T(8,128)(2,1)} async-done(((bf16[1024,768]{1,0:T(8,128)(2,1)}), bf16[128,768]{1,0:T(8,128)(2,1)}) %reduce-scatter.10.cloned.1.call-update) | async-done | bytes 196624 | tf_op jit(solution)/shard_map/reduce_scatter | solution.py:299
  1156.0 36.5 %reduce-scatter.12.cloned.1.call-done = bf16[128,768]{1,0:T(8,128)(2,1)} async-done(((bf16[1024,768]{1,0:T(8,128)(2,1)}), bf16[128,768]{1,0:T(8,128)(2,1)}) %reduce-scatter.12.cloned.1.call-update) | async-done | bytes 196624 | tf_op jit(solution)/shard_map/reduce_scatter | solution.py:305
  1229.3 14.0 reduce-scatter.16.cloned.1.call-done
  1243.3 50.4 %reduce-scatter.18.cloned.1.call-done = bf16[384,768]{1,0:T(8,128)(2,1)} async-done(((bf16[1536,768]{1,0:T(8,128)(2,1)}), bf16[384,768]{1,0:T(8,128)(2,1)}) %reduce-scatter.18.cloned.1.call-update) | async-done | bytes 589840 | tf_op jit(solution)/shard_map/reduce_scatter | solution.py:342
  1293.7 87.5 %reduce-scatter.14.cloned.1.call-done = bf16[384,1536]{1,0:T(8,128)(2,1)} async-done(((bf16[1536,1536]{1,0:T(8,128)(2,1)}), bf16[384,1536]{1,0:T(8,128)(2,1)}) %reduce-scatter.14.cloned.1.call-update) | async-done | bytes 1179664 | tf_op jit(solution)/shard_map/reduce_scatter | solution.py:336
  1381.3 88.5 %reduce-scatter.20.cloned.1.call-done = bf16[384,1536]{1,0:T(8,128)(2,1)} async-done(((bf16[1536,1536]{1,0:T(8,128)(2,1)}), bf16[384,1536]{1,0:T(8,128)(2,1)}) %reduce-scatter.20.cloned.1.call-update) | async-done | bytes 1179664 | tf_op jit(solution)/shard_map/reduce_scatter | solution.py:345
  1469.8 214.6 %reduce-scatter.22.cloned.1.call-done = bf16[384,4096]{1,0:T(8,128)(2,1)} async-done(((bf16[1536,4096]{1,0:T(8,128)(2,1)}), bf16[384,4096]{1,0:T(8,128)(2,1)}) %reduce-scatter.22.cloned.1.call-update) | async-done | bytes 3145744 | tf_op jit(solution)/shard_map/reduce_scatter | solution.py:203
  1684.4 215.1 %reduce-scatter.24.cloned.1.call-done = bf16[384,4096]{1,0:T(8,128)(2,1)} async-done(((bf16[1536,4096]{1,0:T(8,128)(2,1)}), bf16[384,4096]{1,0:T(8,128)(2,1)}) %reduce-scatter.24.cloned.1.call-update) | async-done | bytes 3145744 | tf_op jit(solution)/shard_map/reduce_scatter | solution.py:206
  1899.5 215.1 %reduce-scatter.26.cloned.1.call-done = bf16[1024,1536]{1,0:T(8,128)(2,1)} async-done(((bf16[4096,1536]{1,0:T(8,128)(2,1)}), bf16[1024,1536]{1,0:T(8,128)(2,1)}) %reduce-scatter.26.cloned.1.call-update) | async-done | bytes 3145744 | tf_op jit(solution)/shard_map/reduce_scatter | solution.py:209
  2124.2 11.6 all-reduce.5
  2136.0 12.9 all-reduce.3
  2151.2 148.6 %all-reduce.8.cloned.1.call-done = (bf16[384,1536]{1,0:T(8,128)(2,1)}, bf16[384,768]{1,0:T(8,128)(2,1)}, bf16[384,768]{1,0:T(8,128)(2,1)}, bf16[384,1536]{1,0:T(...) async-done(((bf16[384,1536]{1,0:T(8,128)(2,1)}, bf16[384,768]{1,0:T(8,128)(2,1)}, bf16[384,768]{1,0:T(8,128)(2,1)}, ...) | async-done | bytes 12976144 | tf_op jit(solution)/shard_map/psum | solution.py:363
  (254 shorter events, 147.0 us)
Async XLA Ops:
  7.2 60.0 %copy-start = (f32[1,128,1536]{2,1,0:T(8,128)S(1)}, f32[1,128,1536]{2,1,0:T(8,128)}, u32[]{:S(2)}) copy-start(f32[1,128,1536]{2,1,0:T(8,128)} %param.20) | copy-start | bytes 2359300
  7.2 55.6 %all-gather.18.cloned.1.call-start = ((), (), s32[]{:S(2)}) async-start(), calls=%async_computation.12 | async-start | bytes 2949120 | tf_op jit(solution)/shard_map/all_gather | solution.py:78
  7.9 105.8 %all-gather.12.cloned.1.call-start = ((), (), s32[]{:S(2)}) async-start(), calls=%async_computation.9 | async-start | bytes 2949120 | tf_op jit(solution)/shard_map/all_gather | solution.py:77
  8.7 132.0 %all-gather.20.cloned.1.call-start = ((), (), s32[]{:S(2)}) async-start(), calls=%async_computation.13 | async-start | bytes 1769472 | tf_op jit(solution)/shard_map/all_gather | solution.py:119
  23.0 90.7 %copy-start.38 = (f32[1536]{0:T(1024)}, f32[1536]{0:T(1024)S(1)}, u32[]{:S(2)}) copy-start(f32[1536]{0:T(1024)S(1)} %reshape.263) | copy-start | bytes 18436
  24.8 88.9 %copy-start.40 = (f32[128]{0:T(128)}, f32[128]{0:T(128)S(1)}, u32[]{:S(2)}) copy-start(f32[128]{0:T(128)S(1)} %get-tuple-element.489) | copy-start | bytes 1540
  26.1 87.6 %copy-start.16 = (bf16[128,1536]{1,0:T(8,128)(2,1)}, bf16[128,1536]{1,0:T(8,128)(2,1)S(1)}, u32[]{:S(2)}) copy-start(bf16[128,1536]{1,0:T(8,128)(2,1)S(1)} %multiply_convert_fusion.4) | copy-start | bytes 1179652
  65.7 165.9 %all-gather.16.cloned.1.call-start = ((), (), s32[]{:S(2)}) async-start(), calls=%async_computation.11 | async-start | bytes 5898240 | tf_op jit(solution)/shard_map/all_gather | solution.py:76
  66.2 192.0 %all-gather.14.cloned.1.call-start = ((), (), s32[]{:S(2)}) async-start(), calls=%async_computation.10 | async-start | bytes 1769472 | tf_op jit(solution)/shard_map/all_gather | solution.py:118
  67.4 170.8 %copy-start.8 = (bf16[1,128,1536]{2,1,0:T(8,128)(2,1)}, bf16[1,128,1536]{2,1,0:T(8,128)(2,1)S(1)}, u32[]{:S(2)}) copy-start(bf16[1,128,1536]{2,1,0:T(8,128)(2,1)S(1)} %multiply_convert_fusion.5) | copy-start | bytes 1179652
  119.0 230.1 %all-gather.22.cloned.1.call-start = ((), (), s32[]{:S(2)}) async-start(), calls=%async_computation.14 | async-start | bytes 5898240 | tf_op jit(solution)/shard_map/all_gather | solution.py:79
  119.6 447.8 %all-gather.24.cloned.1.call-start = ((), (), s32[]{:S(2)}) async-start(), calls=%async_computation.15 | async-start | bytes 15728640 | tf_op jit(solution)/shard_map/all_gather | solution.py:163
  120.3 665.1 %all-gather.26.cloned.1.call-start = ((), (), s32[]{:S(2)}) async-start(), calls=%async_computation.16 | async-start | bytes 15728640 | tf_op jit(solution)/shard_map/all_gather | solution.py:164
  121.1 882.3 %all-gather.28.cloned.1.call-start = ((), (), s32[]{:S(2)}) async-start(), calls=%async_computation.17 | async-start | bytes 15728640 | tf_op jit(solution)/shard_map/all_gather | solution.py:165
  121.8 1028.9 %reduce-scatter.10.cloned.1.call-start = ((), (), s32[]{:S(2)}) async-start(), calls=%async_computation.18 | async-start | bytes 1769472 | tf_op jit(solution)/shard_map/reduce_scatter | solution.py:299
  266.8 82.3 %copy-start.14 = (f32[8,2,128,96]{2,3,1,0:T(8,128)}, f32[8,2,128,96]{2,3,1,0:T(8,128)S(1)}, u32[]{:S(2)}) copy-start(f32[8,2,128,96]{2,3,1,0:T(8,128)S(1)} %get-tuple-element.220) | copy-start | bytes 2359300
  266.9 308.2 %copy-start.18 = (bf16[128,8,2,96]{0,3,2,1:T(8,128)(2,1)}, bf16[128,8,2,96]{0,3,2,1:T(8,128)(2,1)S(1)}, u32[]{:S(2)}) copy-start(bf16[128,8,2,96]{0,3,2,1:T(8,128)(2,1)S(1)} %bitcast_convert_fusion) | copy-start | bytes 1179652
  353.1 432.3 %copy-start.10 = (bf16[128,1536]{1,0:T(8,128)(2,1)}, bf16[128,1536]{1,0:T(8,128)(2,1)S(1)}, u32[]{:S(2)}) copy-start(bf16[128,1536]{1,0:T(8,128)(2,1)S(1)} %multiply_convert_fusion.3) | copy-start | bytes 1179652
  794.0 217.5 %copy-start.6 = (bf16[128,4096]{1,0:T(8,128)(2,1)}, bf16[128,4096]{1,0:T(8,128)(2,1)S(1)}, u32[]{:S(2)}) copy-start(bf16[128,4096]{1,0:T(8,128)(2,1)S(1)} %get-tuple-element.494) | copy-start | bytes 3145732
  1003.4 46.9 %copy-start.24 = (f32[1,128,1536]{2,1,0:T(8,128)S(1)}, f32[1,128,1536]{2,1,0:T(8,128)}, u32[]{:S(2)}) copy-start(f32[1,128,1536]{2,1,0:T(8,128)} %param.21) | copy-start | bytes 2359300
  1102.6 49.2 %copy-start.35 = (f32[128,96]{0,1:T(8,128)S(1)}, f32[128,96]{0,1:T(8,128)}, u32[]{:S(2)}) copy-start(f32[128,96]{0,1:T(8,128)} %get-tuple-element.485) | copy-start | bytes 147460
  1102.6 51.1 %copy-start.17 = (bf16[128,1536]{1,0:T(8,128)(2,1)S(1)}, bf16[128,1536]{1,0:T(8,128)(2,1)}, u32[]{:S(2)}) copy-start(bf16[128,1536]{1,0:T(8,128)(2,1)} %copy-done.16) | copy-start | bytes 1179652
  1102.6 89.9 %reduce-scatter.12.cloned.1.call-start = ((), (), s32[]{:S(2)}) async-start(), calls=%async_computation.19 | async-start | bytes 1769472 | tf_op jit(solution)/shard_map/reduce_scatter | solution.py:305
  1103.3 140.0 %reduce-scatter.16.cloned.1.call-start = ((), (), s32[]{:S(2)}) async-start(), calls=%async_computation.21 | async-start | bytes 2949120 | tf_op jit(solution)/shard_map/reduce_scatter | solution.py:339
  1155.9 40.9 %copy-start.32 = (f32[128,96]{0,1:T(8,128)S(1)}, f32[128,96]{0,1:T(8,128)}, u32[]{:S(2)}) copy-start(f32[128,96]{0,1:T(8,128)} %get-tuple-element.487) | copy-start | bytes 147460
  1155.9 137.8 %reduce-scatter.18.cloned.1.call-start = ((), (), s32[]{:S(2)}) async-start(), calls=%async_computation.22 | async-start | bytes 2949120 | tf_op jit(solution)/shard_map/reduce_scatter | solution.py:342
  1195.7 185.6 %reduce-scatter.14.cloned.1.call-start = ((), (), s32[]{:S(2)}) async-start(), calls=%async_computation.20 | async-start | bytes 5898240 | tf_op jit(solution)/shard_map/reduce_scatter | solution.py:336
  1200.6 269.2 %reduce-scatter.20.cloned.1.call-start = ((), (), s32[]{:S(2)}) async-start(), calls=%async_computation.23 | async-start | bytes 5898240 | tf_op jit(solution)/shard_map/reduce_scatter | solution.py:345
  1205.6 478.8 %reduce-scatter.22.cloned.1.call-start = ((), (), s32[]{:S(2)}) async-start(), calls=%async_computation.24 | async-start | bytes 15728640 | tf_op jit(solution)/shard_map/reduce_scatter | solution.py:203
  1213.6 685.9 %reduce-scatter.24.cloned.1.call-start = ((), (), s32[]{:S(2)}) async-start(), calls=%async_computation.25 | async-start | bytes 15728640 | tf_op jit(solution)/shard_map/reduce_scatter | solution.py:206
  1221.3 893.3 %reduce-scatter.26.cloned.1.call-start = ((), (), s32[]{:S(2)}) async-start(), calls=%async_computation.26 | async-start | bytes 15728640 | tf_op jit(solution)/shard_map/reduce_scatter | solution.py:209
  1229.3 1070.6 %all-reduce.8.cloned.1.call-start = ((), (), s32[]{:S(2)}) async-start(), calls=%async_computation.27 | async-start | bytes 25952256 | tf_op jit(solution)/shard_map/psum | solution.py:363
  (34 other events, 188.9 us)
Sparse Core Ops, SparseCore 0:
  9.6 53.1 all-gather.17
  64.4 49.2 all-gather.11
  116.2 24.4 all-gather.19
  142.1 89.4 all-gather.15
  233.9 24.3 all-gather.13
  259.7 89.4 all-gather.21
  350.7 216.6 all-gather.23
  568.9 216.3 all-gather.25
  786.9 216.3 all-gather.27
  1102.7 47.9 reduce-scatter.9
  1154.0 38.4 reduce-scatter.11
  1195.2 48.0 reduce-scatter.15
  1246.2 47.5 reduce-scatter.17
  1296.5 84.7 reduce-scatter.13
  1384.0 85.7 reduce-scatter.19
  1472.0 212.3 reduce-scatter.21
  1686.6 212.8 reduce-scatter.23
  1901.7 212.8 reduce-scatter.25
  2119.6 180.1 all-reduce.7
where the time goes:
time: 2330 us
  waiting for transfers between devices  2030 us (87%)
  matrix products  112 us (5%)
  blocking collectives  89.3 us (4%)
  other arithmetic  36.7 us (2%)
  local copies, waits for them, and re-layouts  34 us (1%)
    reduce_scatter x1, waiting for transfers between devices, local(): lax.psum_scatter(grad_down_full.astype(jnp.bfloat16), 'fsdp', scatter_dim...  215 us
    reduce_scatter x1, waiting for transfers between devices, local(): lax.psum_scatter(grad_up_full.astype(jnp.bfloat16), 'fsdp', scatter_dimen...  215 us
    reduce_scatter x1, waiting for transfers between devices, local(): lax.psum_scatter(grad_gate_full.astype(jnp.bfloat16), 'fsdp', scatter_dim...  215 us
    all_gather x1, waiting for transfers between devices, local(): lax.all_gather(w_gate, 'fsdp', axis=0, tiled=True)  214 us
    all_gather x1, waiting for transfers between devices, local(): lax.all_gather(w_up, 'fsdp', axis=0, tiled=True)  210 us
    all_gather x1, waiting for transfers between devices, local(): lax.all_gather(w_down, 'fsdp', axis=0, tiled=True)  209 us
    psum x1, waiting for transfers between devices, local(): lax.psum(shard_query.astype(jnp.bfloat16), 'ctx').astype(jnp.float32)  149 us
    reduce_scatter x1, waiting for transfers between devices, local(): lax.psum_scatter(grad_out_full.astype(jnp.bfloat16), 'fsdp', scatter_dime...  88.5 us
  transfers between devices with their start and end apart: 19, of which 19 were waited for; matrix products, arithmetic and copies ran while one was open for 4% of the time, Pallas kernels for 0%

commit v1 on v0

v1 whole, which is shorter than its diff:
```python
import jax
import jax.numpy as jnp
from jax import lax
from jax.sharding import PartitionSpec as P

HEADS = 16
KV_HEADS = 8
HEAD_DIM = 96

eps_norm = 1e-05
rope_base = 100000.0
masked_value = -1e30

f32 = jnp.float32
bf16 = jnp.bfloat16


def times(left, right):
    return jnp.dot(left, right, preferred_element_type=f32)


def times_transposed(left, right):
    return lax.dot_general(left, right, (((1,), (1,)), ((), ())), preferred_element_type=f32)


def transposed_times(left, right):
    return lax.dot_general(left, right, (((0,), (0,)), ((), ())), preferred_element_type=f32)


def norm_scale(features):
    return lax.rsqrt(jnp.mean(features * features, axis=-1, keepdims=True) + eps_norm)


def norm_back(upstream, features, row_scale, gain_vector):
    weighted = upstream * gain_vector
    inner_mean = jnp.mean(weighted * features, axis=-1, keepdims=True)
    grad_rows = row_scale * weighted - features * (row_scale * row_scale * row_scale) * inner_mean
    return (grad_rows, jnp.sum(upstream * (features * row_scale), axis=0))


def partner(x, axis, mask):
    return lax.ppermute(x, axis, [(i, i ^ mask) for i in range(lax.axis_size(axis))])


def plane_blocks(x):
    count = lax.axis_size("ctx")
    mine = jnp.stack([x] + [partner(x, "ctx", 2 * s) for s in range(1, count // 2)])
    other = partner(mine, "ctx", 1)
    return jnp.stack([mine, other], axis=1).reshape((count,) + x.shape)


def plane_reduce(parts):
    count = parts.shape[0]
    split = parts.reshape((count // 2, 2) + parts.shape[1:])
    got = partner(split[:, 1], "ctx", 1)
    chip = (split[:, 0].astype(f32) + got.astype(f32)).astype(bf16)
    total = chip[0].astype(f32)
    for s in range(1, count // 2):
        total = total + partner(chip[s], "ctx", 2 * s).astype(f32)
    return total


def butterfly(x, axis):
    mask = 1
    while mask < lax.axis_size(axis):
        x = x + partner(x, axis, mask)
        mask *= 2
    return x


def line_blocks(x):
    return jnp.stack([x] + [partner(x, "fsdp", s) for s in range(1, lax.axis_size("fsdp"))])


def line_reduce(parts):
    total = parts[0].astype(f32)
    for s in range(1, parts.shape[0]):
        total = total + partner(parts[s], "fsdp", s).astype(f32)
    return total


def rope_tables(count):
    half_dim = HEAD_DIM // 2
    frequencies = rope_base ** (-(jnp.arange(half_dim, dtype=f32) * 2.0) / HEAD_DIM)
    angles = jnp.arange(count, dtype=f32)[:, None] * frequencies[None, :]
    angles = jnp.concatenate([angles, angles], axis=-1)[:, None, :]
    return jnp.cos(angles), jnp.sin(angles)


def rotate(features, cosines, sines):
    half_dim = HEAD_DIM // 2
    turned = jnp.concatenate([-features[..., half_dim:], features[..., :half_dim]], axis=-1)
    return features * cosines + turned * sines


def local(
    inputs,
    teacher,
    lengths,
    w_query,
    w_key,
    w_value,
    w_out,
    w_gate,
    w_up,
    w_down,
    gain_attn,
    gain_ffn,
):
    hidden_in = inputs[0]
    target = teacher[0]
    seq_length = lengths[0]
    tokens, width = hidden_in.shape
    C = lax.axis_size("ctx")
    Z = lax.axis_size("fsdp")
    p = lax.axis_index("ctx")
    z = lax.axis_index("fsdp")
    rows_z = width // Z
    seq = C * tokens
    q_heads = HEADS // C
    kv_heads = max(1, KV_HEADS // C)
    kv_copies = max(1, C // KV_HEADS)
    group = q_heads // kv_heads
    q_cols = q_heads * HEAD_DIM
    kv_cols = kv_heads * HEAD_DIM
    ff = w_gate.shape[1]
    ff_piece = ff // (Z * C)
    scale_attn = HEAD_DIM ** (-0.5)
    plane_order = jnp.arange(C, dtype=jnp.int32) ^ p
    line_order = jnp.arange(Z, dtype=jnp.int32) ^ z
    positions = p * tokens + jnp.arange(tokens, dtype=jnp.int32)

    def reorder(x, order):
        return jnp.take(x, order, axis=0)

    def line_columns(x, inverse=False):
        cut = x.reshape(x.shape[0], Z, rows_z)
        return jnp.take(cut, line_order, axis=1).reshape(x.shape)

    gains = reorder(line_blocks(jnp.stack([gain_attn, gain_ffn])), line_order)
    gain_one = gains[:, 0].reshape(width).astype(f32)
    gain_two = gains[:, 1].reshape(width).astype(f32)
    kv_start = (p * KV_HEADS // C) * HEAD_DIM
    qkv_own = jnp.concatenate(
        [
            lax.dynamic_slice_in_dim(w_query, p * q_cols, q_cols, 1),
            lax.dynamic_slice_in_dim(w_key, kv_start, kv_cols, 1),
            lax.dynamic_slice_in_dim(w_value, kv_start, kv_cols, 1),
        ],
        axis=1,
    )
    w_qkv = line_blocks(qkv_own).reshape(width, q_cols + 2 * kv_cols)
    out_cols = width // C
    out_own = lax.dynamic_slice_in_dim(w_out, p * out_cols, out_cols, 1)
    out_mine = reorder(line_blocks(out_own), line_order).reshape(C, q_cols, out_cols)
    out_sent = reorder(out_mine, plane_order)
    out_got = jnp.stack([out_sent[0]] + [partner(out_sent[i], "ctx", i) for i in range(1, C)])
    w_out_rows = reorder(out_got, plane_order).transpose(1, 0, 2).reshape(q_cols, width)

    def ff_columns(w):
        cut = w.reshape(rows_z, Z, C, ff_piece)
        return lax.dynamic_index_in_dim(cut, p, 2, False).reshape(rows_z, Z * ff_piece)

    def ff_rows(w):
        return lax.dynamic_slice_in_dim(w, p * ff_piece, ff_piece, 0)

    ff_own = Z * ff_piece
    gate_up = lax.all_gather(
        jnp.concatenate([ff_columns(w_gate), ff_columns(w_up)], axis=1), "fsdp", axis=0, tiled=True
    )
    w_gate_cols = gate_up[:, :ff_own]
    w_up_cols = gate_up[:, ff_own:]
    w_down_rows = lax.all_gather(ff_rows(w_down), "fsdp", axis=0, tiled=True)
    valid_count = butterfly(lengths.astype(f32), "fsdp")[0]

    scale_one = norm_scale(hidden_in)
    normed_one = (hidden_in * scale_one * gain_one).astype(bf16)
    normed_all = plane_blocks(line_columns(normed_one)).reshape(seq, width)
    qkv = times(normed_all, w_qkv).reshape(C, tokens, q_cols + 2 * kv_cols)
    qkv = reorder(qkv, plane_order).reshape(seq, q_cols + 2 * kv_cols)
    cosines, sines = rope_tables(seq)
    queries = rotate(qkv[:, :q_cols].reshape(seq, q_heads, HEAD_DIM), cosines, sines)
    queries = queries.astype(bf16).reshape(seq, kv_heads, group, HEAD_DIM)
    keys = rotate(
        qkv[:, q_cols : q_cols + kv_cols].reshape(seq, kv_heads, HEAD_DIM), cosines, sines
    ).astype(bf16)
    values = qkv[:, q_cols + kv_cols :].reshape(seq, kv_heads, HEAD_DIM).astype(bf16)
    scores = scale_attn * jnp.einsum(
        "qhgd,khd->hgqk", queries, keys, preferred_element_type=f32
    )
    at = jnp.arange(seq, dtype=jnp.int32)
    allowed = (at[None, :] <= at[:, None]) & (at[None, :] < seq_length)
    scores = jnp.where(allowed, scores, masked_value)
    row_max = jnp.max(scores, axis=-1, keepdims=True)
    weights = jnp.exp(scores - row_max)
    row_sum = jnp.sum(weights, axis=-1, keepdims=True)
    probs = weights / row_sum
    probs_low = probs.astype(bf16)
    attended = jnp.einsum("hgqk,khd->qhgd", probs_low, values, preferred_element_type=f32)
    attended_low = attended.astype(bf16).reshape(seq, q_cols)

    def to_plane(x):
        return reorder(x.reshape((C, tokens) + x.shape[1:]), plane_order)

    attended_plane = to_plane(attended_low).reshape(seq, q_cols)
    mixed = plane_reduce(times(attended_plane, w_out_rows).astype(bf16).reshape(C, tokens, width))
    middle = hidden_in + mixed

    scale_two = norm_scale(middle)
    normed_two = plane_blocks((middle * scale_two * gain_two).astype(bf16)).reshape(seq, width)
    gate_pre = times(normed_two, w_gate_cols)
    up_value = times(normed_two, w_up_cols)
    sigmoid_gate = jax.nn.sigmoid(gate_pre)
    silu_gate = gate_pre * sigmoid_gate
    activated = (silu_gate * up_value).astype(bf16)
    output = middle + plane_reduce(
        times(activated, w_down_rows).astype(bf16).reshape(C, tokens, width)
    )

    valid_rows = (positions < seq_length).astype(f32)
    residual_error = output - target
    squares = jnp.sum(valid_rows[:, None] * residual_error * residual_error)
    loss_value = butterfly(butterfly(squares.reshape(1), "ctx"), "fsdp")[0] / valid_count
    grad_output = valid_rows[:, None] * (2.0 * residual_error) / valid_count

    grad_low = plane_blocks(grad_output.astype(bf16)).reshape(seq, width)
    grad_act = times_transposed(grad_low, w_down_rows)
    grad_gate_pre = (
        grad_act * up_value * (sigmoid_gate * (1.0 + gate_pre * (1.0 - sigmoid_gate)))
    ).astype(bf16)
    grad_up_value = (grad_act * silu_gate).astype(bf16)
    grad_normed_two = plane_reduce(
        (
            times_transposed(grad_gate_pre, w_gate_cols) + times_transposed(grad_up_value, w_up_cols)
        )
        .astype(bf16)
        .reshape(C, tokens, width)
    )
    grad_down = transposed_times(activated, grad_low).astype(bf16)
    grad_gate_up = transposed_times(
        normed_two, jnp.concatenate([grad_gate_pre, grad_up_value], axis=1)
    ).astype(bf16)
    shard_down = lax.psum_scatter(grad_down, "fsdp", scatter_dimension=0, tiled=True)
    shard_gate_up = lax.psum_scatter(grad_gate_up, "fsdp", scatter_dimension=0, tiled=True)
    back_two, grad_gain_two = norm_back(grad_normed_two, middle, scale_two, gain_two)
    grad_middle = grad_output + back_two

    m_low = plane_blocks(grad_middle.astype(bf16)).reshape(seq, width)
    grad_attended = times_transposed(m_low, w_out_rows).astype(bf16)
    grad_out = transposed_times(attended_plane, m_low).astype(bf16)
    grad_attended = reorder(grad_attended.reshape(C, tokens, q_cols), plane_order).reshape(
        seq, kv_heads, group, HEAD_DIM
    )
    row_delta = jnp.einsum("qhgd,qhgd->hgq", grad_attended.astype(f32), attended)
    grad_probs = jnp.einsum(
        "qhgd,khd->hgqk", grad_attended, values, preferred_element_type=f32
    )
    grad_scores = (probs * (grad_probs - row_delta[..., None])).astype(bf16)
    grad_values = jnp.einsum(
        "hgqk,qhgd->khd", probs_low, grad_attended, preferred_element_type=f32
    )
    grad_queries = scale_attn * jnp.einsum(
        "hgqk,khd->qhgd", grad_scores, keys, preferred_element_type=f32
    )
    grad_keys = scale_attn * jnp.einsum(
        "hgqk,qhgd->khd", grad_scores, queries, preferred_element_type=f32
    )
    grad_qkv = jnp.concatenate(
        [
            rotate(grad_queries.reshape(seq, q_heads, HEAD_DIM), cosines, -sines)
            .astype(bf16)
            .reshape(seq, q_cols),
            rotate(grad_keys, cosines, -sines).astype(bf16).reshape(seq, kv_cols),
            grad_values.astype(bf16).reshape(seq, kv_cols),
        ],
        axis=1,
    )
    grad_qkv = to_plane(grad_qkv).reshape(seq, q_cols + 2 * kv_cols)
    grad_w_qkv = transposed_times(normed_all, grad_qkv).astype(bf16)
    grad_normed_one = line_columns(
        plane_reduce(times_transposed(grad_qkv, w_qkv).astype(bf16).reshape(C, tokens, width))
    )
    back_one, grad_gain_one = norm_back(grad_normed_one, hidden_in, scale_one, gain_one)
    grad_hidden = grad_middle + back_one

    shard_qkv = line_reduce(grad_w_qkv.reshape(Z, rows_z, q_cols + 2 * kv_cols)).astype(bf16)
    out_parts = reorder(grad_out.reshape(q_cols, C, out_cols).transpose(1, 0, 2), plane_order)
    out_parts = jnp.stack([out_parts[0]] + [partner(out_parts[i], "ctx", i) for i in range(1, C)])
    out_parts = reorder(out_parts, plane_order).reshape(Z, rows_z, out_cols)
    shard_out = line_reduce(reorder(out_parts, line_order)).astype(bf16)

    ffn_all = reorder(
        plane_blocks(
            jnp.concatenate([shard_gate_up.reshape(-1), shard_down.reshape(-1)]).reshape(-1, width)
        ),
        plane_order,
    ).reshape(C, -1)
    cut = 2 * rows_z * ff_own
    gate_up_all = ffn_all[:, :cut].reshape(C, rows_z, 2, Z, ff_piece)
    gate_up_all = gate_up_all.transpose(2, 1, 3, 0, 4).reshape(2, rows_z, ff).astype(f32)
    down_all = ffn_all[:, cut:].reshape(C * ff_piece, width).astype(f32)
    attn_all = reorder(plane_blocks(jnp.concatenate([shard_qkv, shard_out], axis=1)), plane_order)
    attn_all = attn_all.astype(f32).transpose(1, 0, 2)
    final_query = attn_all[:, :, :q_cols].reshape(rows_z, width)

    def kv_final(start):
        part = attn_all[:, :, start : start + kv_cols]
        part = part.reshape(rows_z, C // kv_copies, kv_copies, kv_cols)
        return jnp.sum(part, axis=2).reshape(rows_z, KV_HEADS * HEAD_DIM)

    final_key = kv_final(q_cols)
    final_value = kv_final(q_cols + kv_cols)
    final_out = attn_all[:, :, q_cols + 2 * kv_cols :].reshape(rows_z, width)

    def gain_final(grad):
        whole = butterfly(grad.reshape(Z, rows_z), "ctx")
        return line_reduce(reorder(whole, line_order))

    return (
        output[None],
        loss_value,
        grad_hidden[None],
        final_query,
        final_key,
        final_value,
        final_out,
        gate_up_all[0],
        gate_up_all[1],
        down_all,
        gain_final(grad_gain_one),
        gain_final(grad_gain_two),
    )


def solution(mesh):
    return jax.shard_map(
        local,
        mesh=mesh,
        in_specs=(
            P("fsdp", "ctx", None),
            P("fsdp", "ctx", None),
            P("fsdp"),
            P("fsdp", None),
            P("fsdp", None),
            P("fsdp", None),
            P("fsdp", None),
            P("fsdp", None),
            P("fsdp", None),
            P("fsdp", None),
            P("fsdp"),
            P("fsdp"),
        ),
        out_specs=(
            P("fsdp", "ctx", None),
            P(),
            P("fsdp", "ctx", None),
            P("fsdp", None),
            P("fsdp", None),
            P("fsdp", None),
            P("fsdp", None),
            P("fsdp", None),
            P("fsdp", None),
            P("fsdp", None),
            P("fsdp"),
            P("fsdp"),
        ),
        check_vma=False,
    )
```

time: 2330 us -> 764 us (0.33)
  waiting for transfers between devices: 2030 us -> 226 us
  local copies, waits for them, and re-layouts: 34 us -> 212 us
  starting transfers between devices: 0.76 us -> 113 us
  blocking collectives: 89.3 us -> 0 us
  other arithmetic: 36.7 us -> 118 us
  matrix products: 112 us -> 63.9 us
    reduce_scatter x9 -> x2, waiting for transfers between devices: 968 us -> 0.01 us  [the longest x1 0.01 us: local(): lax.psum_scatter(grad_down, 'fsdp', scatter_dimension=0, tiled=True)]
    all_gather x9 -> x2, waiting for transfers between devices: 909 us -> 30.6 us  [the longest x1 28 us: local(): w_down_rows = lax.all_gather(ff_rows(w_down), 'fsdp', axis=0, tiled=True)]
    ppermute x0 -> x88, waiting for transfers between devices: none -> 196 us  [partner(): lax.ppermute(x, axis, [(i, i ^ mask) for i in range(lax.axis_size(axis))])]
    psum x1 -> x0, waiting for transfers between devices: 149 us -> none  [local(): lax.psum(shard_query.astype(jnp.bfloat16), 'ctx').astype(jnp.float32)]
    ppermute x0 -> x88, starting transfers between devices: none -> 113 us  [partner(): lax.ppermute(x, axis, [(i, i ^ mask) for i in range(lax.axis_size(axis))])]
    unnamed x100 -> x204, local copies, waits for them, and re-layouts: 11.5 us -> 71.7 us
    psum x2 -> x0, blocking collectives: 51.7 us -> none  [the longest x1 38.8 us: local(): lax.psum((squares, jnp.sum(valid_rows)), ('ctx', 'fsdp'))]
    another operation x2 -> x20, other arithmetic: 0.01 us -> 44.3 us  [the longest x12 37.4 us: plane_blocks(): return jnp.stack([mine, other], axis=1).reshape((count,) + x.shape)]
  transfers between devices with their start and end apart: 19 -> 92, of which waited for: 19 -> 52; matrix products, arithmetic and copies ran while one was open for 4% -> 30% of each run, Pallas kernels for 0% -> 0%
where the time goes in v1:
time: 764 us; the launch traced here: 757 us
  waiting for transfers between devices  226 us (30%)
  local copies, waits for them, and re-layouts  212 us (28%)
  other arithmetic  118 us (15%)
  starting transfers between devices  113 us (15%)
  matrix products  63.9 us (8%)
  between operations  23.1 us (3%)
    ppermute x88, waiting for transfers between devices, partner(): lax.ppermute(x, axis, [(i, i ^ mask) for i in range(lax.axis_size(axis))])  196 us
    ppermute x88, starting transfers between devices, partner(): lax.ppermute(x, axis, [(i, i ^ mask) for i in range(lax.axis_size(axis))])  113 us
    unnamed x204, local copies, waits for them, and re-layouts  71.7 us
    gather x16, local copies, waits for them, and re-layouts, reorder(): return jnp.take(x, order, axis=0)  40.2 us
    another operation x12, other arithmetic, plane_blocks(): return jnp.stack([mine, other], axis=1).reshape((count,) + x.shape)  37.4 us
    all_gather x1, waiting for transfers between devices, local(): w_down_rows = lax.all_gather(ff_rows(w_down), 'fsdp', axis=0, tiled=True)  28 us
    dot_general x5, matrix products, times(): return jnp.dot(left, right, preferred_element_type=f32)  19 us
    another operation x5, local copies, waits for them, and re-layouts, plane_blocks(): return jnp.stack([mine, other], axis=1).reshape((count,) + x.shape)  17.2 us
  transfers between devices with their start and end apart: 92, of which 52 were waited for; matrix products, arithmetic and copies ran while one was open for 30% of the time, Pallas kernels for 0%

profile of v1, /device:TPU:0, one launch (start us, length us, event | category | flops | bytes accessed | tf_op | source)
XLA Modules:
  0.0 756.6 jit_solution(8398249595243926156)
XLA Ops:
  174.0 7.4 collective-permute-done.21
  181.4 9.2 %collective-permute-done.22 = bf16[128,1536]{0,1:T(8,128)(2,1)} collective-permute-done((bf16[128,1536]{0,1:T(8,128)(2,1)}, bf16[128,1536]{0,1:T(8,128)(2,1)}, u32[]{:S(2)}, u32[]{:S(2)}) %collective-permute-start.22) | collective-permute-done | bytes 393248 | tf_op jit(solution)/shard_map/ppermute | solution.py:42
  197.1 8.3 %collective-permute-done.24 = bf16[128,1536]{0,1:T(8,128)(2,1)S(1)} collective-permute-done((bf16[128,1536]{0,1:T(8,128)(2,1)S(1)}, bf16[128,1536]{0,1:T(8,128)(2,1)S(1)}, u32[]{:S(2)}, u32[]{:S(2)}) %collective-permute-start.24) | collective-permute-done | bytes 393248 | tf_op jit(solution)/shard_map/ppermute | solution.py:42
  205.4 8.1 %collective-permute-done.25 = bf16[128,1536]{0,1:T(8,128)(2,1)S(1)} collective-permute-done((bf16[128,1536]{0,1:T(8,128)(2,1)S(1)}, bf16[128,1536]{0,1:T(8,128)(2,1)S(1)}, u32[]{:S(2)}, u32[]{:S(2)}) %collective-permute-start.25) | collective-permute-done | bytes 393248 | tf_op jit(solution)/shard_map/ppermute | solution.py:42
  236.0 28.0 %all-gather.5.cloned.1.call-done = bf16[512,1536]{1,0:T(8,128)(2,1)} async-done(((bf16[128,1536]{1,0:T(8,128)(2,1)}), bf16[512,1536]{1,0:T(8,128)(2,1)}) %all-gather.5.cloned.1.call-update) | async-done | bytes 1572880 | tf_op jit(solution)/shard_map/all_gather | solution.py:173
  289.3 8.3 %collective-permute-done.30 = bf16[128,1536]{0,1:T(8,128)(2,1)} collective-permute-done((bf16[128,1536]{0,1:T(8,128)(2,1)}, bf16[128,1536]{0,1:T(8,128)(2,1)}, u32[]{:S(2)}, u32[]{:S(2)}) %collective-permute-start.30) | collective-permute-done | bytes 393248 | tf_op jit(solution)/shard_map/ppermute | solution.py:42
  302.8 8.6 %collective-permute-done.39 = bf16[128,1536]{0,1:T(8,128)(2,1)S(1)} collective-permute-done((bf16[128,1536]{0,1:T(8,128)(2,1)S(1)}, bf16[128,1536]{0,1:T(8,128)(2,1)S(1)}, u32[]{:S(2)}, u32[]{:S(2)}) %collective-permute-start.39) | collective-permute-done | bytes 393248 | tf_op jit(solution)/shard_map/ppermute | solution.py:42
  311.4 7.6 %collective-permute-done.40 = bf16[128,1536]{0,1:T(8,128)(2,1)S(1)} collective-permute-done((bf16[128,1536]{0,1:T(8,128)(2,1)S(1)}, bf16[128,1536]{0,1:T(8,128)(2,1)S(1)}, u32[]{:S(2)}, u32[]{:S(2)}) %collective-permute-start.40) | collective-permute-done | bytes 393248 | tf_op jit(solution)/shard_map/ppermute | solution.py:42
  329.5 6.2 multiply_convert_fusion
  357.3 5.7 collective-permute-done.44
  363.0 8.0 %collective-permute-done.45 = bf16[128,1536]{0,1:T(8,128)(2,1)} collective-permute-done((bf16[128,1536]{0,1:T(8,128)(2,1)}, bf16[128,1536]{0,1:T(8,128)(2,1)}, u32[]{:S(2)}, u32[]{:S(2)}) %collective-permute-start.45) | collective-permute-done | bytes 393248 | tf_op jit(solution)/shard_map/ppermute | solution.py:42
  380.1 8.6 %collective-permute-done.47 = bf16[128,1536]{0,1:T(8,128)(2,1)S(1)} collective-permute-done((bf16[128,1536]{0,1:T(8,128)(2,1)S(1)}, bf16[128,1536]{0,1:T(8,128)(2,1)S(1)}, u32[]{:S(2)}, u32[]{:S(2)}) %collective-permute-start.47) | collective-permute-done | bytes 393248 | tf_op jit(solution)/shard_map/ppermute | solution.py:42
  389.3 6.7 collective-permute-done.49
  403.0 6.2 convolution_convert_fusion.3
  438.3 5.7 fusion.5
  513.5 8.7 %collective-permute-start.67 = (bf16[384,192]{0,1:T(8,128)(2,1)}, bf16[384,192]{0,1:T(8,128)(2,1)}, u32[]{:S(2)}, u32[]{:S(2)}) collective-permute-start(bf16[384,192]{0,1:T(8,128)(2,1)} %get-tuple-element.147), channel_id=1, source_target_pairs={{0,3},{1,2},{2,1},{3,0},{4,7},{5,6},{6,5},{7,4},{8,11},{9,10},{10,... | collective-permute-start | bytes 442376 | tf_op jit(solution)/shard_map/ppermute | solution.py:42
  525.8 5.3 collective-permute-start.73
  532.3 6.0 collective-permute-start.36
  547.2 7.8 %collective-permute-done.72 = bf16[384,1536]{1,0:T(8,128)(2,1)} collective-permute-done((bf16[384,1536]{1,0:T(8,128)(2,1)}, bf16[384,1536]{1,0:T(8,128)(2,1)}, u32[]{:S(2)}, u32[]{:S(2)}) %collective-permute-start.72) | collective-permute-done | bytes 1179680 | tf_op jit(solution)/shard_map/ppermute | solution.py:42
  555.0 30.5 %collective-permute-done.73 = bf16[384,1536]{1,0:T(8,128)(2,1)} collective-permute-done((bf16[384,1536]{1,0:T(8,128)(2,1)}, bf16[384,1536]{1,0:T(8,128)(2,1)}, u32[]{:S(2)}, u32[]{:S(2)}) %collective-permute-start.73) | collective-permute-done | bytes 1179680 | tf_op jit(solution)/shard_map/ppermute | solution.py:42
  587.8 6.4 fusion.103
  607.5 8.9 %collective-permute-done.53 = bf16[128,1536]{0,1:T(8,128)(2,1)} collective-permute-done((bf16[128,1536]{0,1:T(8,128)(2,1)}, bf16[128,1536]{0,1:T(8,128)(2,1)}, u32[]{:S(2)}, u32[]{:S(2)}) %collective-permute-start.53) | collective-permute-done | bytes 393248 | tf_op jit(solution)/shard_map/ppermute | solution.py:42
  629.0 5.3 collective-permute-start.85
  671.6 8.3 %pad_maximum_fusion = bf16[4,2,384,1536]{3,2,1,0:T(8,128)(2,1)} fusion(bf16[4,1,384,1536]{3,2,1,0:T(8,128)(2,1)} %bitcast.183, bf16[4,1,384,1536]{3,2,1,0:T(8,128)(2,1)} %get-tuple-element.88), kind=kLoop, calls=%fused_computation.18 | loop fusion | flops 4718592 | bytes 18874368 | tf_op jit(solution)/shard_map/stack | solution.py:49
  679.9 9.1 %gather_fusion.6 = bf16[8,384,1536]{2,1,0:T(8,128)(2,1)} fusion(bf16[8,384,1536]{2,1,0:T(8,128)(2,1)} %bitcast.501, s32[1024]{0:T(1024)} %pad_clamp_fusion.2), kind=kCustom, calls=%fused_computation.16 | custom fusion | bytes 18874400 | tf_op jit(solution)/shard_map/jit(_take)/gather | solution.py:134
  689.0 12.6 %copy.258 = bf16[1,8,384,1536]{3,1,2,0:T(8,128)(2,1)} copy(bf16[1,8,384,1536]{3,2,1,0:T(8,128)(2,1)} %bitcast.502) | data formatting | bytes 18874368
  701.6 5.4 broadcast_select_fusion
  710.4 6.2 copy_bitcast_fusion
  716.6 10.9 %fusion.107 = (f32[1,384,4,8,128]{4,3,2,1,0:T(8,128)}, f32[1,384,4,8,128]{4,3,2,1,0:T(8,128)}) fusion(f32[2,384,4,8,128]{4,3,2,1,0:T(8,128)} %copy_bitcast_fusion), kind=kLoop, calls=%fused_computation.310 | loop fusion | bytes 25165824 | tf_op jit(solution)/shard_map/slice | solution.py:328
  727.5 7.1 squeeze.201
  734.6 7.1 squeeze.202
  741.8 6.8 reshape.712
  (563 shorter events, 448.8 us)
Async XLA Ops:
  7.2 219.5 %all-gather.3.cloned.1.call-start = ((), (), s32[]{:S(2)}) async-start(), calls=%async_computation.2 | async-start | bytes 3932160 | tf_op jit(solution)/shard_map/all_gather | solution.py:168
  8.8 29.0 %collective-permute-start = (bf16[2,384]{1,0:T(2,128)(2,1)S(1)}, bf16[2,384]{1,0:T(2,128)(2,1)S(1)}, u32[]{:S(2)}, u32[]{:S(2)}) collective-permute-start(bf16[2,384]{1,0:T(2,128)(2,1)S(1)} %pad_maximum_fusion.21), channel_id=1, source_target_pairs={{0,1},{1,0},{2,3},{3,2},{4,5},{5,4},{6,7},{7,6},{8,9},{9,8},{10,11... | collective-permute-start | bytes 4616 | tf_op jit(solution)/shard_map/ppermute | solution.py:42
  11.9 26.0 %collective-permute-start.1 = (bf16[2,384]{1,0:T(2,128)(2,1)S(1)}, bf16[2,384]{1,0:T(2,128)(2,1)S(1)}, u32[]{:S(2)}, u32[]{:S(2)}) collective-permute-start(bf16[2,384]{1,0:T(2,128)(2,1)S(1)} %pad_maximum_fusion.21), channel_id=1, source_target_pairs={{0,2},{1,3},{2,0},{3,1},{4,6},{5,7},{6,4},{7,5},{8,10},{9,11},{10,... | collective-permute-start | bytes 4616 | tf_op jit(solution)/shard_map/ppermute | solution.py:42
  14.5 23.9 %collective-permute-start.2 = (bf16[2,384]{1,0:T(2,128)(2,1)S(1)}, bf16[2,384]{1,0:T(2,128)(2,1)S(1)}, u32[]{:S(2)}, u32[]{:S(2)}) collective-permute-start(bf16[2,384]{1,0:T(2,128)(2,1)S(1)} %pad_maximum_fusion.21), channel_id=1, source_target_pairs={{0,3},{1,2},{2,1},{3,0},{4,7},{5,6},{6,5},{7,4},{8,11},{9,10},{10,... | collective-permute-start | bytes 4616 | tf_op jit(solution)/shard_map/ppermute | solution.py:42
  16.3 29.4 %collective-permute-start.10 = (bf16[384,192]{1,0:T(8,128)(2,1)}, bf16[384,192]{1,0:T(8,128)(2,1)}, u32[]{:S(2)}, u32[]{:S(2)}) collective-permute-start(bf16[384,192]{1,0:T(8,128)(2,1)} %constant_dynamic-slice_fusion.3), channel_id=1, source_target_pairs={{0,1},{1,0},{2,3},{3,2},{4,5},{5,4},{6,7},{7,6},{8,9},{9,8},{10,11... | collective-permute-start | bytes 442376 | tf_op jit(solution)/shard_map/ppermute | solution.py:42
  17.2 30.0 %collective-permute-start.11 = (bf16[384,192]{1,0:T(8,128)(2,1)}, bf16[384,192]{1,0:T(8,128)(2,1)}, u32[]{:S(2)}, u32[]{:S(2)}) collective-permute-start(bf16[384,192]{1,0:T(8,128)(2,1)} %constant_dynamic-slice_fusion.3), channel_id=1, source_target_pairs={{0,2},{1,3},{2,0},{3,1},{4,6},{5,7},{6,4},{7,5},{8,10},{9,11},{10,... | collective-permute-start | bytes 442376 | tf_op jit(solution)/shard_map/ppermute | solution.py:42
  37.9 64.7 %collective-permute-start.7 = (bf16[384,384]{1,0:T(8,128)(2,1)}, bf16[384,384]{1,0:T(8,128)(2,1)}, u32[]{:S(2)}, u32[]{:S(2)}) collective-permute-start(bf16[384,384]{1,0:T(8,128)(2,1)} %pad_maximum_fusion.19), channel_id=1, source_target_pairs={{0,1},{1,0},{2,3},{3,2},{4,5},{5,4},{6,7},{7,6},{8,9},{9,8},{10,11... | collective-permute-start | bytes 884744 | tf_op jit(solution)/shard_map/ppermute | solution.py:42
  44.2 21.1 %collective-permute-start.3 = (bf16[128,1536]{0,1:T(8,128)(2,1)}, bf16[128,1536]{0,1:T(8,128)(2,1)}, u32[]{:S(2)}, u32[]{:S(2)}) collective-permute-start(bf16[128,1536]{0,1:T(8,128)(2,1)} %bitcast_select_fusion.3), channel_id=1, source_target_pairs={{0,8},{4,12},{8,0},{12,4},{16,24},{20,28},{24,16},{28,20},{1,9},{5... | collective-permute-start | bytes 1179656 | tf_op jit(solution)/shard_map/ppermute | solution.py:42
  45.7 19.7 %collective-permute-start.4 = (bf16[128,1536]{0,1:T(8,128)(2,1)}, bf16[128,1536]{0,1:T(8,128)(2,1)}, u32[]{:S(2)}, u32[]{:S(2)}) collective-permute-start(bf16[128,1536]{0,1:T(8,128)(2,1)} %bitcast_select_fusion.3), channel_id=1, source_target_pairs={{0,16},{4,20},{8,24},{12,28},{16,0},{20,4},{24,8},{28,12},{1,17},{... | collective-permute-start | bytes 1179656 | tf_op jit(solution)/shard_map/ppermute | solution.py:42
  47.2 19.8 %collective-permute-start.5 = (bf16[128,1536]{0,1:T(8,128)(2,1)}, bf16[128,1536]{0,1:T(8,128)(2,1)}, u32[]{:S(2)}, u32[]{:S(2)}) collective-permute-start(bf16[128,1536]{0,1:T(8,128)(2,1)} %bitcast_select_fusion.3), channel_id=1, source_target_pairs={{0,24},{4,28},{8,16},{12,20},{16,8},{20,12},{24,0},{28,4},{1,25},{... | collective-permute-start | bytes 1179656 | tf_op jit(solution)/shard_map/ppermute | solution.py:42
  61.0 41.6 %collective-permute-start.8 = (bf16[384,384]{1,0:T(8,128)(2,1)}, bf16[384,384]{1,0:T(8,128)(2,1)}, u32[]{:S(2)}, u32[]{:S(2)}) collective-permute-start(bf16[384,384]{1,0:T(8,128)(2,1)} %pad_maximum_fusion.19), channel_id=1, source_target_pairs={{0,2},{1,3},{2,0},{3,1},{4,6},{5,7},{6,4},{7,5},{8,10},{9,11},{10,... | collective-permute-start | bytes 884744 | tf_op jit(solution)/shard_map/ppermute | solution.py:42
  65.3 37.3 %collective-permute-start.9 = (bf16[384,384]{1,0:T(8,128)(2,1)}, bf16[384,384]{1,0:T(8,128)(2,1)}, u32[]{:S(2)}, u32[]{:S(2)}) collective-permute-start(bf16[384,384]{1,0:T(8,128)(2,1)} %pad_maximum_fusion.19), channel_id=1, source_target_pairs={{0,3},{1,2},{2,1},{3,0},{4,7},{5,6},{6,5},{7,4},{8,11},{9,10},{10,... | collective-permute-start | bytes 884744 | tf_op jit(solution)/shard_map/ppermute | solution.py:42
  70.2 34.8 %collective-permute-start.6 = (bf16[4,128,1536]{1,2,0:T(8,128)(2,1)}, bf16[4,128,1536]{1,2,0:T(8,128)(2,1)}, u32[]{:S(2)}, u32[]{:S(2)}) collective-permute-start(bf16[4,128,1536]{1,2,0:T(8,128)(2,1)} %get-tuple-element.122), channel_id=1, source_target_pairs={{0,4},{4,0},{8,12},{12,8},{16,20},{20,16},{24,28},{28,24},{1,5},{5... | collective-permute-start | bytes 4718600 | tf_op jit(solution)/shard_map/ppermute | solution.py:42
  161.9 102.1 %all-gather.5.cloned.1.call-start = ((), (), s32[]{:S(2)}) async-start(), calls=%async_computation.3 | async-start | bytes 1966080 | tf_op jit(solution)/shard_map/all_gather | solution.py:173
  170.6 20.0 %collective-permute-start.22 = (bf16[128,1536]{0,1:T(8,128)(2,1)}, bf16[128,1536]{0,1:T(8,128)(2,1)}, u32[]{:S(2)}, u32[]{:S(2)}) collective-permute-start(bf16[128,1536]{0,1:T(8,128)(2,1)} %get-tuple-element.120), channel_id=1, source_target_pairs={{0,16},{4,20},{8,24},{12,28},{16,0},{20,4},{24,8},{28,12},{1,17},{... | collective-permute-start | bytes 1179656 | tf_op jit(solution)/shard_map/ppermute | solution.py:42
  216.2 209.1 %reduce-scatter.5.cloned.1.call-start = ((), (), s32[]{:S(2)}) async-start(), calls=%async_computation.5 | async-start | bytes 1966080 | tf_op jit(solution)/shard_map/reduce_scatter | solution.py:243
  357.2 146.9 %reduce-scatter.3.cloned.1.call-start = ((), (), s32[]{:S(2)}) async-start(), calls=%async_computation.4 | async-start | bytes 3932160 | tf_op jit(solution)/shard_map/reduce_scatter | solution.py:244
  397.9 29.7 %collective-permute-start.50 = (bf16[4,128,1536]{1,2,0:T(8,128)(2,1)}, bf16[4,128,1536]{1,2,0:T(8,128)(2,1)}, u32[]{:S(2)}, u32[]{:S(2)}) collective-permute-start(bf16[4,128,1536]{1,2,0:T(8,128)(2,1)} %get-tuple-element.106), channel_id=1, source_target_pairs={{0,4},{4,0},{8,12},{12,8},{16,20},{20,16},{24,28},{28,24},{1,5},{5... | collective-permute-start | bytes 4718600 | tf_op jit(solution)/shard_map/ppermute | solution.py:42
  402.1 22.5 %collective-permute-start.83 = (f32[4,384]{1,0:T(4,128)}, f32[4,384]{1,0:T(4,128)}, u32[]{:S(2)}, u32[]{:S(2)}) collective-permute-start(f32[4,384]{1,0:T(4,128)} %add.329), channel_id=1, source_target_pairs={{0,8},{4,12},{8,0},{12,4},{16,24},{20,28},{24,16},{28,20},{1,9},{5... | collective-permute-start | bytes 18440 | tf_op jit(solution)/shard_map/ppermute | solution.py:42
  459.6 81.1 %collective-permute-start.51 = (bf16[4,128,1536]{1,2,0:T(8,128)(2,1)}, bf16[4,128,1536]{1,2,0:T(8,128)(2,1)}, u32[]{:S(2)}, u32[]{:S(2)}) collective-permute-start(bf16[4,128,1536]{1,2,0:T(8,128)(2,1)} %bitcast.546), channel_id=1, source_target_pairs={{0,4},{4,0},{8,12},{12,8},{16,20},{20,16},{24,28},{28,24},{1,5},{5... | collective-permute-start | bytes 4718600 | tf_op jit(solution)/shard_map/ppermute | solution.py:42
  474.0 51.7 %collective-permute-start.55 = (bf16[384,384]{0,1:T(8,128)(2,1)}, bf16[384,384]{0,1:T(8,128)(2,1)}, u32[]{:S(2)}, u32[]{:S(2)}) collective-permute-start(bf16[384,384]{0,1:T(8,128)(2,1)} %get-tuple-element.123), channel_id=1, source_target_pairs={{0,1},{1,0},{2,3},{3,2},{4,5},{5,4},{6,7},{7,6},{8,9},{9,8},{10,11... | collective-permute-start | bytes 884744 | tf_op jit(solution)/shard_map/ppermute | solution.py:42
  474.6 56.5 %collective-permute-start.56 = (bf16[384,384]{0,1:T(8,128)(2,1)}, bf16[384,384]{0,1:T(8,128)(2,1)}, u32[]{:S(2)}, u32[]{:S(2)}) collective-permute-start(bf16[384,384]{0,1:T(8,128)(2,1)} %get-tuple-element.125), channel_id=1, source_target_pairs={{0,2},{1,3},{2,0},{3,1},{4,6},{5,7},{6,4},{7,5},{8,10},{9,11},{10,... | collective-permute-start | bytes 884744 | tf_op jit(solution)/shard_map/ppermute | solution.py:42
  509.8 22.5 %collective-permute-start.57 = (bf16[384,384]{0,1:T(8,128)(2,1)S(1)}, bf16[384,384]{0,1:T(8,128)(2,1)}, u32[]{:S(2)}, u32[]{:S(2)}) collective-permute-start(bf16[384,384]{0,1:T(8,128)(2,1)S(1)} %get-tuple-element.124), channel_id=1, source_target_pairs={{0,3},{1,2},{2,1},{3,0},{4,7},{5,6},{6,5},{7,4},{8,11},{9,10},{10,... | collective-permute-start | bytes 884744 | tf_op jit(solution)/shard_map/ppermute | solution.py:42
  525.8 29.2 %collective-permute-start.72 = (bf16[384,1536]{1,0:T(8,128)(2,1)}, bf16[384,1536]{1,0:T(8,128)(2,1)}, u32[]{:S(2)}, u32[]{:S(2)}) collective-permute-start(bf16[384,1536]{1,0:T(8,128)(2,1)} %reshape.697), channel_id=1, source_target_pairs={{0,8},{4,12},{8,0},{12,4},{16,24},{20,28},{24,16},{28,20},{1,9},{5... | collective-permute-start | bytes 3538952 | tf_op jit(solution)/shard_map/ppermute | solution.py:42
  525.8 59.7 %collective-permute-start.73 = (bf16[384,1536]{1,0:T(8,128)(2,1)}, bf16[384,1536]{1,0:T(8,128)(2,1)}, u32[]{:S(2)}, u32[]{:S(2)}) collective-permute-start(bf16[384,1536]{1,0:T(8,128)(2,1)} %reshape.697), channel_id=1, source_target_pairs={{0,16},{4,20},{8,24},{12,28},{16,0},{20,4},{24,8},{28,12},{1,17},{... | collective-permute-start | bytes 3538952 | tf_op jit(solution)/shard_map/ppermute | solution.py:42
  531.1 54.4 %collective-permute-start.74 = (bf16[384,1536]{1,0:T(8,128)(2,1)}, bf16[384,1536]{1,0:T(8,128)(2,1)}, u32[]{:S(2)}, u32[]{:S(2)}) collective-permute-start(bf16[384,1536]{1,0:T(8,128)(2,1)} %reshape.697), channel_id=1, source_target_pairs={{0,24},{4,28},{8,16},{12,20},{16,8},{20,12},{24,0},{28,4},{1,25},{... | collective-permute-start | bytes 3538952 | tf_op jit(solution)/shard_map/ppermute | solution.py:42
  532.3 61.9 %collective-permute-start.36 = (f32[1]{0:T(128)}, f32[1]{0:T(128)}, u32[]{:S(2)}, u32[]{:S(2)}) collective-permute-start(f32[1]{0:T(128)} %add.298), channel_id=1, source_target_pairs={{0,2},{1,3},{2,0},{3,1},{4,6},{5,7},{6,4},{7,5},{8,10},{9,11},{10,... | collective-permute-start | bytes 20 | tf_op jit(solution)/shard_map/ppermute | solution.py:42
  540.7 54.6 %collective-permute-start.84 = (f32[4,384]{1,0:T(4,128)S(1)}, f32[4,384]{1,0:T(4,128)S(1)}, u32[]{:S(2)}, u32[]{:S(2)}) collective-permute-start(f32[4,384]{1,0:T(4,128)S(1)} %add.330), channel_id=1, source_target_pairs={{0,16},{4,20},{8,24},{12,28},{16,0},{20,4},{24,8},{28,12},{1,17},{... | collective-permute-start | bytes 18440 | tf_op jit(solution)/shard_map/ppermute | solution.py:42
  555.0 41.5 %collective-permute-start.68 = (bf16[384,576]{0,1:T(8,128)(2,1)}, bf16[384,576]{0,1:T(8,128)(2,1)}, u32[]{:S(2)}, u32[]{:S(2)}) collective-permute-start(bf16[384,576]{0,1:T(8,128)(2,1)} %get-tuple-element.150), channel_id=1, source_target_pairs={{0,8},{4,12},{8,0},{12,4},{16,24},{20,28},{24,16},{28,20},{1,9},{5... | collective-permute-start | bytes 1327112 | tf_op jit(solution)/shard_map/ppermute | solution.py:42
  594.2 77.4 %collective-permute-start.75 = (bf16[4,384,1536]{2,1,0:T(8,128)(2,1)}, bf16[4,384,1536]{2,1,0:T(8,128)(2,1)}, u32[]{:S(2)}, u32[]{:S(2)}) collective-permute-start(bf16[4,384,1536]{2,1,0:T(8,128)(2,1)} %get-tuple-element.89), channel_id=1, source_target_pairs={{0,4},{4,0},{8,12},{12,8},{16,20},{20,16},{24,28},{28,24},{1,5},{5... | collective-permute-start | bytes 14155784 | tf_op jit(solution)/shard_map/ppermute | solution.py:42
  596.5 20.0 %collective-permute-start.53 = (bf16[128,1536]{0,1:T(8,128)(2,1)}, bf16[128,1536]{0,1:T(8,128)(2,1)}, u32[]{:S(2)}, u32[]{:S(2)}) collective-permute-start(bf16[128,1536]{0,1:T(8,128)(2,1)} %get-tuple-element.104), channel_id=1, source_target_pairs={{0,16},{4,20},{8,24},{12,28},{16,0},{20,4},{24,8},{28,12},{1,17},{... | collective-permute-start | bytes 1179656 | tf_op jit(solution)/shard_map/ppermute | solution.py:42
  607.0 39.3 %collective-permute-start.71 = (bf16[4,384,576]{1,2,0:T(8,128)(2,1)}, bf16[4,384,576]{1,2,0:T(8,128)(2,1)}, u32[]{:S(2)}, u32[]{:S(2)}) collective-permute-start(bf16[4,384,576]{1,2,0:T(8,128)(2,1)} %get-tuple-element.101), channel_id=1, source_target_pairs={{0,4},{4,0},{8,12},{12,8},{16,20},{20,16},{24,28},{28,24},{1,5},{5... | collective-permute-start | bytes 5308424 | tf_op jit(solution)/shard_map/ppermute | solution.py:42
  (142 other events, 1401.0 us)
Sparse Core Ops, SparseCore 0:
  162.0 64.6 all-gather.2
  228.3 35.6 all-gather.4
  357.3 32.9 reduce-scatter.4
  409.3 58.1 reduce-scatter.2

commit v2 on v1

v2 whole, which is shorter than its diff:
```python
import functools

import jax
import jax.numpy as jnp
from jax import lax
from jax.experimental import pallas as pl
from jax.experimental.pallas import tpu as pltpu
from jax.sharding import PartitionSpec as P

HEADS = 16
KV_HEADS = 8
HEAD_DIM = 96
LANES = 128

eps_norm = 1e-05
rope_base = 100000.0
masked_value = -1e30

f32 = jnp.float32
bf16 = jnp.bfloat16

VMEM = pl.BlockSpec(memory_space=pltpu.VMEM)
SMEM = pl.BlockSpec(memory_space=pltpu.SMEM)
ANY = pl.BlockSpec(memory_space=pl.ANY)
KERNEL_VMEM = 56 * 1024 * 1024


def times(left, right):
    return jnp.dot(left, right, preferred_element_type=f32)


def times_transposed(left, right):
    return lax.dot_general(left, right, (((1,), (1,)), ((), ())), preferred_element_type=f32)


def transposed_times(left, right):
    return lax.dot_general(left, right, (((0,), (0,)), ((), ())), preferred_element_type=f32)


def norm_scale(features):
    return lax.rsqrt(jnp.mean(features * features, axis=-1, keepdims=True) + eps_norm)


def norm_back(upstream, features, row_scale, gain_vector):
    weighted = upstream * gain_vector
    inner_mean = jnp.mean(weighted * features, axis=-1, keepdims=True)
    grad_rows = row_scale * weighted - features * (row_scale * row_scale * row_scale) * inner_mean
    return (grad_rows, jnp.sum(upstream * (features * row_scale), axis=0))


def partner(x, axis, mask):
    return lax.ppermute(x, axis, [(i, i ^ mask) for i in range(lax.axis_size(axis))])


def plane_blocks(x):
    blocks = []
    for s in range(lax.axis_size("ctx") // 2):
        mine = partner(x, "ctx", 2 * s) if s else x
        blocks += [mine, partner(mine, "ctx", 1)]
    return blocks


def plane_reduce(keep, give):
    sent = []
    for s in range(len(keep) - 1, 0, -1):
        chip = keep[s].astype(f32) + partner(give[s], "ctx", 1).astype(f32)
        sent.append(partner(chip.astype(bf16), "ctx", 2 * s))
    total = keep[0].astype(f32) + partner(give[0], "ctx", 1).astype(f32)
    for got in sent:
        total = total + got.astype(f32)
    return total


def tree_sum(x, axis):
    mask = 1
    while mask < lax.axis_size(axis):
        x = x + partner(x, axis, mask)
        mask *= 2
    return x


def line_blocks(x):
    return [x] + [partner(x, "fsdp", s) for s in range(1, lax.axis_size("fsdp"))]


def line_reduce(parts):
    total = parts[0].astype(f32)
    for s in range(1, len(parts)):
        total = total + partner(parts[s], "fsdp", s).astype(f32)
    return total


def pick(x, index, axis=0):
    return lax.dynamic_index_in_dim(x, index, axis, False)


def unsort(blocks, me):
    stacked = jnp.stack(blocks)
    return [pick(stacked, me ^ b) for b in range(len(blocks))]


def rope_tables(count):
    half_dim = HEAD_DIM // 2
    frequencies = rope_base ** (-(jnp.arange(half_dim, dtype=f32) * 2.0) / HEAD_DIM)
    angles = jnp.arange(count, dtype=f32)[:, None] * frequencies[None, :]
    cosines, sines = jnp.cos(angles), jnp.sin(angles)
    pad = jnp.zeros((count, LANES - HEAD_DIM), f32)
    return (
        jnp.concatenate([cosines, cosines, pad], axis=1),
        jnp.concatenate([-sines, sines, pad], axis=1),
    )


def turned(x):
    lane = lax.broadcasted_iota(jnp.int32, x.shape, 1)
    half_dim = HEAD_DIM // 2
    return jnp.where(
        lane < half_dim, pltpu.roll(x, LANES - half_dim, 1), pltpu.roll(x, half_dim, 1)
    )


def head_of(x, head):
    if head:
        x = pltpu.roll(x, x.shape[1] - head * HEAD_DIM, 1)
    return x[:, :LANES]


def packed(heads):
    wide = -(-len(heads) * HEAD_DIM // LANES) * LANES
    total = None
    for index, head in enumerate(heads):
        if wide > LANES:
            head = jnp.concatenate([head, jnp.zeros((head.shape[0], wide - LANES), f32)], axis=1)
        if index:
            head = pltpu.roll(head, index * HEAD_DIM, 1)
        total = head if total is None else total + head
    return total


def attention_forward_kernel(C, tokens, q_heads, kv_heads, block, info_ref, *refs):
    n_refs = refs[:C]
    w_ref, cos_ref, sin_ref = refs[C : C + 3]
    n_all_ref, qkv_ref, att_ref, lse_ref = refs[C + 3 : C + 7]
    keep_refs = refs[C + 7 : C + 7 + C // 2]
    give_refs = refs[C + 7 + C // 2 : C + 7 + C]
    lin_ref = refs[C + 7 + C]
    me, length = info_ref[0], info_ref[1]
    seq = C * tokens
    group = q_heads // kv_heads
    width_low = q_heads * HEAD_DIM
    for i in range(C):
        n_all_ref[i * tokens : (i + 1) * tokens, :] = n_refs[i][...]
    step = 4 * tokens
    for start in range(0, seq, step):
        lin_ref[start : start + step, :] = times(n_all_ref[start : start + step, :], w_ref[...])
    lane = lax.broadcasted_iota(jnp.int32, (tokens, LANES), 1)
    for i in range(C):
        rows = pl.ds(pl.multiple_of((me ^ i) * tokens, tokens), tokens)
        lin = lin_ref[i * tokens : (i + 1) * tokens, :]
        cosines, sines = cos_ref[rows, :], sin_ref[rows, :]
        for head in range(q_heads + 2 * kv_heads):
            x = head_of(lin, head)
            if head < q_heads + kv_heads:
                x = x * cosines + turned(x) * sines
            else:
                x = jnp.where(lane < HEAD_DIM, x, 0.0)
            qkv_ref[rows, head * LANES : (head + 1) * LANES] = x.astype(bf16)
    scale = HEAD_DIM ** (-0.5)
    for head in range(q_heads):
        k_at = (q_heads + head // group) * LANES
        v_at = k_at + kv_heads * LANES
        for start in range(0, seq, block):
            end = start + block
            q = qkv_ref[start:end, head * LANES : (head + 1) * LANES]
            scores = times_transposed(q, qkv_ref[:end, k_at : k_at + LANES]) * scale
            row = start + lax.broadcasted_iota(jnp.int32, (block, end), 0)
            col = lax.broadcasted_iota(jnp.int32, (block, end), 1)
            scores = jnp.where((col <= row) & (col < length), scores, masked_value)
            row_max = jnp.max(scores, axis=1, keepdims=True)
            weights = jnp.exp(scores - row_max)
            row_sum = jnp.sum(weights, axis=1, keepdims=True)
            probs = (weights * (1.0 / row_sum)).astype(bf16)
            att_ref[start:end, head * LANES : (head + 1) * LANES] = times(
                probs, qkv_ref[:end, v_at : v_at + LANES]
            )
            lse_ref[start:end, head : head + 1] = row_max + jnp.log(row_sum)
    for i in range(C):
        rows = pl.ds(pl.multiple_of((me ^ i) * tokens, tokens), tokens)
        x = att_ref[rows, :]
        low = packed([x[:, h * LANES : (h + 1) * LANES] for h in range(q_heads)])
        (give_refs if i % 2 else keep_refs)[i // 2][...] = low[:, :width_low].astype(bf16)


def attention_forward(blocks, w_qkv, tables, me, length, q_heads, kv_heads):
    C = len(blocks)
    tokens, width = blocks[0].shape
    seq = C * tokens
    heads = q_heads + 2 * kv_heads
    part = jax.ShapeDtypeStruct((tokens, q_heads * HEAD_DIM), bf16)
    result = pl.pallas_call(
        functools.partial(attention_forward_kernel, C, tokens, q_heads, kv_heads, 2 * tokens),
        out_shape=[
            jax.ShapeDtypeStruct((seq, width), bf16),
            jax.ShapeDtypeStruct((seq, heads * LANES), bf16),
            jax.ShapeDtypeStruct((seq, q_heads * LANES), f32),
            jax.ShapeDtypeStruct((seq, LANES), f32),
        ]
        + [part] * C,
        in_specs=[SMEM] + [VMEM] * (C + 3),
        out_specs=[VMEM] * (C + 4),
        scratch_shapes=[pltpu.VMEM((seq, w_qkv.shape[1]), f32)],
        compiler_params=pltpu.CompilerParams(vmem_limit_bytes=KERNEL_VMEM),
        name="attention_forward",
    )(jnp.stack([me, length]).astype(jnp.int32), *blocks, w_qkv, *tables)
    return result[:4], result[4 : 4 + C // 2], result[4 + C // 2 :]


def attention_backward_kernel(C, tokens, q_heads, kv_heads, block, info_ref, *refs):
    grad_refs = refs[:C]
    qkv_ref, att_ref, lse_ref, w_ref, cos_ref, sin_ref = refs[C : C + 6]
    dqkv_ref = refs[C + 6]
    keep_refs = refs[C + 7 : C + 7 + C // 2]
    give_refs = refs[C + 7 + C // 2 : C + 7 + C]
    wide_ref, grad_ref, dq_ref, dkv_ref = refs[C + 7 + C :]
    me, length = info_ref[0], info_ref[1]
    seq = C * tokens
    group = q_heads // kv_heads
    width_low = q_heads * HEAD_DIM
    lane = lax.broadcasted_iota(jnp.int32, (tokens, LANES), 1)
    wide_ref[...] = jnp.zeros_like(wide_ref)
    for i in range(C):
        rows = pl.ds(pl.multiple_of((me ^ i) * tokens, tokens), tokens)
        wide_ref[:, :width_low] = grad_refs[i][...].astype(f32)
        wide = wide_ref[...]
        for head in range(q_heads):
            x = jnp.where(lane < HEAD_DIM, head_of(wide, head), 0.0)
            grad_ref[rows, head * LANES : (head + 1) * LANES] = x.astype(bf16)
    dkv_ref[...] = jnp.zeros_like(dkv_ref)
    scale = HEAD_DIM ** (-0.5)
    for start in range(0, seq, block):
        end = start + block
        lane_b = lax.broadcasted_iota(jnp.int32, (block, LANES), 1)
        delta = jnp.zeros((block, LANES), f32)
        for head in range(q_heads):
            at = slice(head * LANES, (head + 1) * LANES)
            one = jnp.sum(
                grad_ref[start:end, at].astype(f32) * att_ref[start:end, at], axis=1, keepdims=True
            )
            delta = jnp.where(lane_b == head, one, delta)
        delta_t = delta.T
        lse_t = lse_ref[start:end, :].T
        key = lax.broadcasted_iota(jnp.int32, (end, block), 0)
        query = start + lax.broadcasted_iota(jnp.int32, (end, block), 1)
        allowed = (key <= query) & (key < length)
        for head in range(q_heads):
            at = slice(head * LANES, (head + 1) * LANES)
            kv = head // group
            k_at = slice((q_heads + kv) * LANES, (q_heads + kv + 1) * LANES)
            v_at = slice((q_heads + kv_heads + kv) * LANES, (q_heads + kv_heads + kv + 1) * LANES)
            q, grad = qkv_ref[start:end, at], grad_ref[start:end, at]
            k, v = qkv_ref[:end, k_at], qkv_ref[:end, v_at]
            scores = times_transposed(k, q) * scale
            probs = jnp.where(allowed, jnp.exp(scores - lse_t[head : head + 1, :]), 0.0)
            grad_probs = times_transposed(v, grad)
            grad_scores = (probs * (grad_probs - delta_t[head : head + 1, :])).astype(bf16)
            dq_ref[start:end, at] = transposed_times(grad_scores, k) * scale
            dk_at = slice(kv * LANES, (kv + 1) * LANES)
            dv_at = slice((kv_heads + kv) * LANES, (kv_heads + kv + 1) * LANES)
            dkv_ref[:end, dk_at] += times(grad_scores, q) * scale
            dkv_ref[:end, dv_at] += times(probs.astype(bf16), grad)
    for i in range(C):
        rows = pl.ds(pl.multiple_of((me ^ i) * tokens, tokens), tokens)
        cosines, sines = cos_ref[rows, :], sin_ref[rows, :]
        heads = []
        for head in range(q_heads + 2 * kv_heads):
            if head < q_heads:
                x = dq_ref[rows, head * LANES : (head + 1) * LANES]
            else:
                x = dkv_ref[rows, (head - q_heads) * LANES : (head - q_heads + 1) * LANES]
            if head < q_heads + kv_heads:
                x = x * cosines - turned(x) * sines
            heads.append(x)
        dqkv_ref[i * tokens : (i + 1) * tokens, :] = packed(heads).astype(bf16)
    step = 4
    for first in range(0, C, step):
        part = times_transposed(dqkv_ref[first * tokens : (first + step) * tokens, :], w_ref[...])
        for i in range(first, first + step):
            at = (i - first) * tokens
            (give_refs if i % 2 else keep_refs)[i // 2][...] = part[at : at + tokens, :].astype(bf16)


def attention_backward(grads, saved, w_qkv, tables, me, length, q_heads, kv_heads):
    C = len(grads)
    tokens = grads[0].shape[0]
    seq = C * tokens
    width, cols = w_qkv.shape
    part = jax.ShapeDtypeStruct((tokens, width), bf16)
    wide = -(-q_heads * HEAD_DIM // LANES) * LANES
    result = pl.pallas_call(
        functools.partial(attention_backward_kernel, C, tokens, q_heads, kv_heads, 2 * tokens),
        out_shape=[jax.ShapeDtypeStruct((seq, cols), bf16)] + [part] * C,
        in_specs=[SMEM] + [VMEM] * (C + 6),
        out_specs=[VMEM] * (C + 1),
        scratch_shapes=[
            pltpu.VMEM((tokens, wide), f32),
            pltpu.VMEM((seq, q_heads * LANES), bf16),
            pltpu.VMEM((seq, q_heads * LANES), f32),
            pltpu.VMEM((seq, 2 * kv_heads * LANES), f32),
        ],
        compiler_params=pltpu.CompilerParams(vmem_limit_bytes=KERNEL_VMEM),
        name="attention_backward",
    )(jnp.stack([me, length]).astype(jnp.int32), *grads, *saved, w_qkv, *tables)
    return result[0], result[1 : 1 + C // 2], result[1 + C // 2 :]


def ffn_forward_kernel(C, tokens, *refs):
    n_refs = refs[:C]
    gu_ref, down_ref = refs[C : C + 2]
    n_all_ref, act_ref, coef_ref = refs[C + 2 : C + 5]
    keep_refs = refs[C + 5 : C + 5 + C // 2]
    give_refs = refs[C + 5 + C // 2 :]
    own = down_ref.shape[0]
    for i in range(C):
        n_all_ref[i * tokens : (i + 1) * tokens, :] = n_refs[i][...]
    step = 4
    for first in range(0, C, step):
        rows = slice(first * tokens, (first + step) * tokens)
        both = times(n_all_ref[rows, :], gu_ref[...])
        gate, up = both[:, :own], both[:, own:]
        sigmoid = jax.nn.sigmoid(gate)
        silu = gate * sigmoid
        act = (silu * up).astype(bf16)
        act_ref[rows, :] = act
        coef_ref[rows, :own] = (up * (sigmoid * (1.0 + gate * (1.0 - sigmoid)))).astype(bf16)
        coef_ref[rows, own:] = silu.astype(bf16)
        part = times(act, down_ref[...])
        for i in range(first, first + step):
            at = (i - first) * tokens
            (give_refs if i % 2 else keep_refs)[i // 2][...] = part[at : at + tokens, :].astype(bf16)


def ffn_forward(blocks, gate_up, down):
    C = len(blocks)
    tokens, width = blocks[0].shape
    seq, own = C * tokens, down.shape[0]
    part = jax.ShapeDtypeStruct((tokens, width), bf16)
    result = pl.pallas_call(
        functools.partial(ffn_forward_kernel, C, tokens),
        out_shape=[
            jax.ShapeDtypeStruct((seq, width), bf16),
            jax.ShapeDtypeStruct((seq, own), bf16),
            jax.ShapeDtypeStruct((seq, 2 * own), bf16),
        ]
        + [part] * C,
        in_specs=[VMEM] * (C + 2),
        out_specs=[VMEM] * (C + 3),
        compiler_params=pltpu.CompilerParams(vmem_limit_bytes=KERNEL_VMEM),
        name="ffn_forward",
    )(*blocks, gate_up, down)
    return result[:3], result[3 : 3 + C // 2], result[3 + C // 2 :]


def ffn_backward_kernel(C, tokens, *refs):
    g_refs = refs[:C]
    gu_ref, down_ref, coef_ref = refs[C : C + 3]
    g_all_ref, dgu_ref = refs[C + 3 : C + 5]
    keep_refs = refs[C + 5 : C + 5 + C // 2]
    give_refs = refs[C + 5 + C // 2 :]
    own = down_ref.shape[0]
    for i in range(C):
        g_all_ref[i * tokens : (i + 1) * tokens, :] = g_refs[i][...]
    step = 4
    for first in range(0, C, step):
        rows = slice(first * tokens, (first + step) * tokens)
        grad_act = times_transposed(g_all_ref[rows, :], down_ref[...])
        dgu_ref[rows, :own] = (grad_act * coef_ref[rows, :own].astype(f32)).astype(bf16)
        dgu_ref[rows, own:] = (grad_act * coef_ref[rows, own:].astype(f32)).astype(bf16)
        part = times_transposed(dgu_ref[rows, :], gu_ref[...])
        for i in range(first, first + step):
            at = (i - first) * tokens
            (give_refs if i % 2 else keep_refs)[i // 2][...] = part[at : at + tokens, :].astype(bf16)


def ffn_backward(blocks, gate_up, down, coef):
    C = len(blocks)
    tokens, width = blocks[0].shape
    seq, own = C * tokens, down.shape[0]
    part = jax.ShapeDtypeStruct((tokens, width), bf16)
    result = pl.pallas_call(
        functools.partial(ffn_backward_kernel, C, tokens),
        out_shape=[
            jax.ShapeDtypeStruct((seq, width), bf16),
            jax.ShapeDtypeStruct((seq, 2 * own), bf16),
        ]
        + [part] * C,
        in_specs=[VMEM] * (C + 3),
        out_specs=[VMEM] * (C + 2),
        compiler_params=pltpu.CompilerParams(vmem_limit_bytes=KERNEL_VMEM),
        name="ffn_backward",
    )(*blocks, gate_up, down, coef)
    return result[:2], result[2 : 2 + C // 2], result[2 + C // 2 :]


def ffn_slices_kernel(Z, piece, me_ref, gate_ref, up_ref, down_ref, gu_ref, rows_ref, sems):
    me = me_ref[0]
    stride = gate_ref.shape[1] // Z
    copies = []
    for a, ref in enumerate((gate_ref, up_ref)):
        for zz in range(Z):
            at = pl.multiple_of(zz * stride + me * piece, piece)
            copies.append((ref.at[:, pl.ds(at, piece)], gu_ref.at[:, pl.ds((a * Z + zz) * piece, piece)]))
    at = pl.multiple_of(me * piece, piece)
    copies.append((down_ref.at[pl.ds(at, piece), :], rows_ref))
    copies = [pltpu.make_async_copy(a, b, sems.at[n]) for n, (a, b) in enumerate(copies)]
    for copy in copies:
        copy.start()
    for copy in copies:
        copy.wait()


def ffn_slices(w_gate, w_up, w_down, me, C, Z):
    rows, ff = w_gate.shape
    piece = ff // (Z * C)
    if piece % LANES:
        cut = [pick(w.reshape(rows, Z, C, piece), me, 2).reshape(rows, -1) for w in (w_gate, w_up)]
        return jnp.concatenate(cut, axis=1), lax.dynamic_slice_in_dim(w_down, me * piece, piece, 0)
    return pl.pallas_call(
        functools.partial(ffn_slices_kernel, Z, piece),
        out_shape=[
            jax.ShapeDtypeStruct((rows, 2 * Z * piece), bf16),
            jax.ShapeDtypeStruct((piece, w_down.shape[1]), bf16),
        ],
        in_specs=[SMEM, ANY, ANY, ANY],
        out_specs=[ANY, ANY],
        scratch_shapes=[pltpu.SemaphoreType.DMA((2 * Z + 1,))],
        name="ffn_slices",
    )(me.reshape(1), w_gate, w_up, w_down)


def ffn_grads_kernel(C, Z, piece, me_ref, *refs):
    gu_refs, rows_refs = refs[:C], refs[C : 2 * C]
    gate_ref, up_ref, down_ref, wide_ref, tall_ref, sems = refs[2 * C :]
    me = me_ref[0]
    stride = gate_ref.shape[1] // Z
    flying = [None, None]
    for i in range(C):
        slot = i % 2
        for copy in flying[slot] or ():
            copy.wait()
        owner = me ^ i
        wide_ref[slot] = gu_refs[i][...].astype(f32)
        tall_ref[slot] = rows_refs[i][...].astype(f32)
        copies = []
        for a, ref in enumerate((gate_ref, up_ref)):
            for zz in range(Z):
                at = pl.multiple_of(zz * stride + owner * piece, piece)
                copies.append(
                    pltpu.make_async_copy(
                        wide_ref.at[slot, :, pl.ds((a * Z + zz) * piece, piece)],
                        ref.at[:, pl.ds(at, piece)],
                        sems.at[slot, a * Z + zz],
                    )
                )
        at = pl.multiple_of(owner * piece, piece)
        copies.append(
            pltpu.make_async_copy(
                tall_ref.at[slot], down_ref.at[pl.ds(at, piece), :], sems.at[slot, 2 * Z]
            )
        )
        for copy in copies:
            copy.start()
        flying[slot] = copies
    for copies in flying:
        for copy in copies or ():
            copy.wait()


def ffn_grads(gu_blocks, row_blocks, me, Z):
    C = len(gu_blocks)
    rows, cols = gu_blocks[0].shape
    piece, width = row_blocks[0].shape
    ff = C * cols // 2
    if piece % LANES:
        gu = jnp.stack(unsort(gu_blocks, me)).astype(f32).reshape(C, rows, 2, Z, piece)
        gu = gu.transpose(2, 1, 3, 0, 4).reshape(2, rows, ff)
        return gu[0], gu[1], jnp.concatenate(unsort(row_blocks, me), axis=0).astype(f32)
    return pl.pallas_call(
        functools.partial(ffn_grads_kernel, C, Z, piece),
        out_shape=[
            jax.ShapeDtypeStruct((rows, ff), f32),
            jax.ShapeDtypeStruct((rows, ff), f32),
            jax.ShapeDtypeStruct((C * piece, width), f32),
        ],
        in_specs=[SMEM] + [VMEM] * (2 * C),
        out_specs=[ANY] * 3,
        scratch_shapes=[
            pltpu.VMEM((2, rows, cols), f32),
            pltpu.VMEM((2, piece, width), f32),
            pltpu.SemaphoreType.DMA((2, 2 * Z + 1)),
        ],
        compiler_params=pltpu.CompilerParams(vmem_limit_bytes=KERNEL_VMEM),
        name="ffn_grads",
    )(me.reshape(1), *gu_blocks, *row_blocks)


def local(
    inputs,
    teacher,
    lengths,
    w_query,
    w_key,
    w_value,
    w_out,
    w_gate,
    w_up,
    w_down,
    gain_attn,
    gain_ffn,
):
    hidden_in = inputs[0]
    target = teacher[0]
    seq_length = lengths[0]
    tokens, width = hidden_in.shape
    C = lax.axis_size("ctx")
    Z = lax.axis_size("fsdp")
    R = C // 2
    p = lax.axis_index("ctx")
    z = lax.axis_index("fsdp")
    chip, core = p // 2, p % 2
    rows_z = width // Z
    seq = C * tokens
    q_heads = HEADS // C
    kv_heads = max(1, KV_HEADS // C)
    kv_copies = max(1, C // KV_HEADS)
    q_cols = q_heads * HEAD_DIM
    kv_cols = kv_heads * HEAD_DIM
    qkv_cols = q_cols + 2 * kv_cols
    positions = p * tokens + jnp.arange(tokens, dtype=jnp.int32)

    def line_columns(x):
        cut = x.reshape(x.shape[0], Z, rows_z)
        return jnp.concatenate([pick(cut, z ^ i, 1) for i in range(Z)], axis=1)

    gains = jnp.stack(unsort(line_blocks(jnp.stack([gain_attn, gain_ffn])), z))
    gain_one = gains[:, 0].reshape(width).astype(f32)
    gain_two = gains[:, 1].reshape(width).astype(f32)
    gate_up_own, down_own = ffn_slices(w_gate, w_up, w_down, p, C, Z)
    gate_up = lax.all_gather(gate_up_own, "fsdp", axis=0, tiled=True)
    down_rows = lax.all_gather(down_own, "fsdp", axis=0, tiled=True)
    kv_start = (p * KV_HEADS // C) * HEAD_DIM
    qkv_own = jnp.concatenate(
        [
            lax.dynamic_slice_in_dim(w_query, p * q_cols, q_cols, 1),
            lax.dynamic_slice_in_dim(w_key, kv_start, kv_cols, 1),
            lax.dynamic_slice_in_dim(w_value, kv_start, kv_cols, 1),
            jnp.zeros((rows_z, -qkv_cols % LANES), bf16),
        ],
        axis=1,
    )
    w_qkv = jnp.concatenate(line_blocks(qkv_own), axis=0)

    scale_one = norm_scale(hidden_in)
    normed_one = (hidden_in * scale_one * gain_one).astype(bf16)
    normed_blocks = plane_blocks(line_columns(normed_one))
    tables = rope_tables(seq)
    (normed_all, qkv, attended, lse), att_keep, att_give = attention_forward(
        normed_blocks, w_qkv, tables, p, seq_length, q_heads, kv_heads
    )

    out_piece = rows_z // C
    out_own = lax.dynamic_slice_in_dim(w_out, p * out_piece, out_piece, 0)
    out_line = jnp.stack(unsort(line_blocks(out_own), z))
    out_all = jnp.stack(unsort(plane_blocks(out_line), p), axis=1).reshape(width, width)
    valid_count = tree_sum(lengths.astype(f32), "fsdp")[0]

    def heads_of_chip(own, other):
        return jnp.where(
            core == 0,
            jnp.concatenate([own, other], axis=1),
            jnp.concatenate([other, own], axis=1),
        )

    pairs = []
    for s in range(R):
        pair = heads_of_chip(att_keep[s], partner(att_give[s], "ctx", 1))
        pairs.append(partner(pair, "ctx", 2 * s) if s else pair)
    attended_tokens = jnp.concatenate(unsort(pairs, chip), axis=1)
    middle = hidden_in + times(attended_tokens, out_all)

    scale_two = norm_scale(middle)
    normed_two_blocks = plane_blocks((middle * scale_two * gain_two).astype(bf16))
    (normed_two, activated, coef), keep, give = ffn_forward(normed_two_blocks, gate_up, down_rows)
    output = middle + plane_reduce(keep, give)

    valid_rows = (positions < seq_length).astype(f32)
    residual_error = output - target
    squares = jnp.sum(valid_rows[:, None] * residual_error * residual_error)
    grad_output = valid_rows[:, None] * (2.0 * residual_error) / valid_count

    grad_blocks = plane_blocks(grad_output.astype(bf16))
    (grad_low, grad_gu), keep, give = ffn_backward(grad_blocks, gate_up, down_rows, coef)
    grad_normed_two = plane_reduce(keep, give)
    grad_down = transposed_times(activated, grad_low).astype(bf16)
    grad_gate_up = transposed_times(normed_two, grad_gu).astype(bf16)
    shard_down = lax.psum_scatter(grad_down, "fsdp", scatter_dimension=0, tiled=True)
    shard_gate_up = lax.psum_scatter(grad_gate_up, "fsdp", scatter_dimension=0, tiled=True)
    back_two, grad_gain_two = norm_back(grad_normed_two, middle, scale_two, gain_two)
    grad_middle = grad_output + back_two

    m_low = grad_middle.astype(bf16)
    grad_attended = times_transposed(m_low, out_all).astype(bf16)
    cut = grad_attended.reshape(tokens, R, 2 * q_cols)
    blocks = []
    for s in range(R):
        pair = pick(cut, chip ^ s, 1)
        pair = partner(pair, "ctx", 2 * s) if s else pair
        own = jnp.where(core == 0, pair[:, :q_cols], pair[:, q_cols:])
        other = jnp.where(core == 0, pair[:, q_cols:], pair[:, :q_cols])
        blocks += [own, partner(other, "ctx", 1)]
    grad_qkv, keep, give = attention_backward(
        blocks, (qkv, attended, lse), w_qkv, tables, p, seq_length, q_heads, kv_heads
    )
    grad_normed_one = line_columns(plane_reduce(keep, give))
    back_one, grad_gain_one = norm_back(grad_normed_one, hidden_in, scale_one, gain_one)
    grad_hidden = grad_middle + back_one

    grad_out = transposed_times(attended_tokens, m_low).astype(bf16).reshape(Z, C, out_piece, width)
    grad_out = [pick(grad_out, p ^ i, 1).reshape(Z * out_piece, width) for i in range(C)]
    grad_out = plane_reduce(grad_out[0::2], grad_out[1::2]).astype(bf16)
    grad_out = grad_out.reshape(Z, out_piece, width)
    shard_out = line_reduce([pick(grad_out, z ^ i) for i in range(Z)]).astype(bf16)
    grad_w_qkv = transposed_times(normed_all, grad_qkv).astype(bf16)
    shard_qkv = line_reduce(
        [grad_w_qkv[i * rows_z : (i + 1) * rows_z] for i in range(Z)]
    ).astype(bf16)

    final_gate, final_up, final_down = ffn_grads(
        plane_blocks(shard_gate_up), plane_blocks(shard_down), p, Z
    )
    final_out = jnp.concatenate(unsort(plane_blocks(shard_out), p), axis=0).astype(f32)
    qkv_all = unsort(plane_blocks(shard_qkv), p)
    final_query = jnp.concatenate([part[:, :q_cols] for part in qkv_all], axis=1).astype(f32)

    def kv_final(start):
        parts = [part[:, start : start + kv_cols].astype(f32) for part in qkv_all]
        parts = [sum(parts[n : n + kv_copies]) for n in range(0, C, kv_copies)]
        return jnp.concatenate(parts, axis=1)

    final_key = kv_final(q_cols)
    final_value = kv_final(q_cols + kv_cols)

    loss_value = tree_sum(tree_sum(squares.reshape(1), "ctx"), "fsdp")[0] / valid_count

    def gain_final(grad):
        whole = tree_sum(grad.reshape(Z, rows_z), "ctx")
        return line_reduce([pick(whole, z ^ i) for i in range(Z)])

    return (
        output[None],
        loss_value,
        grad_hidden[None],
        final_query,
        final_key,
        final_value,
        final_out,
        final_gate,
        final_up,
        final_down,
        gain_final(grad_gain_one),
        gain_final(grad_gain_two),
    )


def solution(mesh):
    return jax.shard_map(
        local,
        mesh=mesh,
        in_specs=(
            P("fsdp", "ctx", None),
            P("fsdp", "ctx", None),
            P("fsdp"),
            P("fsdp", None),
            P("fsdp", None),
            P("fsdp", None),
            P("fsdp", None),
            P("fsdp", None),
            P("fsdp", None),
            P("fsdp", None),
            P("fsdp"),
            P("fsdp"),
        ),
        out_specs=(
            P("fsdp", "ctx", None),
            P(),
            P("fsdp", "ctx", None),
            P("fsdp", None),
            P("fsdp", None),
            P("fsdp", None),
            P("fsdp", None),
            P("fsdp", None),
            P("fsdp", None),
            P("fsdp", None),
            P("fsdp"),
            P("fsdp"),
        ),
        check_vma=False,
    )
```

time: 764 us -> 614 us (0.80)
  local copies, waits for them, and re-layouts: 212 us -> 43.1 us
  Pallas kernels: 0 us -> 103 us
  other arithmetic: 118 us -> 50.8 us
  matrix products: 63.9 us -> 21.2 us
  waiting for transfers between devices: 226 us -> 243 us
    pallas_call x0 -> x6, Pallas kernels: none -> 103 us  [the longest x1 36.9 us: ffn_slices(): pl.pallas_call(functools.partial(ffn_slices_kernel, Z, piece), out_shape=...]
    unnamed x204 -> x231, local copies, waits for them, and re-layouts: 71.7 us -> 22.8 us
    ppermute x88 -> x132, waiting for transfers between devices: 196 us -> 243 us  [partner(): lax.ppermute(x, axis, [(i, i ^ mask) for i in range(lax.axis_size(axis))])]
    gather x20 -> x0, local copies, waits for them, and re-layouts: 43.8 us -> none  [the longest x16 40.2 us: reorder(): return jnp.take(x, order, axis=0)]
    another operation x20 -> x8, other arithmetic: 44.3 us -> 3.12 us  [the longest x4 1.81 us: unsort(): stacked = jnp.stack(blocks)]
    all_gather x2, waiting for transfers between devices: 30.6 us -> 0.01 us  [the longest x1 0.01 us: local(): down_rows = lax.all_gather(down_own, 'fsdp', axis=0, tiled=True)]
    another operation x13 -> x7, local copies, waits for them, and re-layouts: 25 us -> 0.84 us  [the longest x4 0.78 us: unsort(): stacked = jnp.stack(blocks)]
    squeeze x9 -> x3, local copies, waits for them, and re-layouts: 20.6 us -> 0.15 us  [pick(): return lax.dynamic_index_in_dim(x, index, axis, False)]
  transfers between devices with their start and end apart: 92 -> 136, of which waited for: 52 -> 46; matrix products, arithmetic and copies ran while one was open for 30% -> 16% of each run, Pallas kernels for 0% -> 4%
where the time goes in v2:
time: 614 us; the launch traced here: 604 us
  waiting for transfers between devices  243 us (40%)
  starting transfers between devices  120 us (20%)
  Pallas kernels  103 us (17%)
  other arithmetic  50.8 us (8%)
  local copies, waits for them, and re-layouts  43.1 us (7%)
  between operations  22.8 us (4%)
  matrix products  21.2 us (3%)
    ppermute x132, waiting for transfers between devices, partner(): lax.ppermute(x, axis, [(i, i ^ mask) for i in range(lax.axis_size(axis))])  243 us
    ppermute x132, starting transfers between devices, partner(): lax.ppermute(x, axis, [(i, i ^ mask) for i in range(lax.axis_size(axis))])  120 us
    pallas_call x1, Pallas kernels, ffn_slices(): pl.pallas_call(functools.partial(ffn_slices_kernel, Z, piece), out_shape=...  36.9 us
    unnamed x231, local copies, waits for them, and re-layouts  22.8 us
    pallas_call x1, Pallas kernels, ffn_backward(): pl.pallas_call(functools.partial(ffn_backward_kernel, C, tokens), out_sha...  22.3 us
    dot_general x4, matrix products, transposed_times(): lax.dot_general(left, right, (((0,), (0,)), ((), ())), preferred_element_...  16.3 us
  transfers between devices with their start and end apart: 136, of which 46 were waited for; matrix products, arithmetic and copies ran while one was open for 16% of the time, Pallas kernels for 4%

profile of v2, /device:TPU:0, one launch (start us, length us, event | category | flops | bytes accessed | tf_op | source)
XLA Modules:
  0.0 604.1 jit_solution(6368173850704271247)
XLA Ops:
  7.3 36.9 %ffn_slices.1 = (bf16[384,1024]{1,0:T(8,128)(2,1)}, bf16[128,1536]{1,0:T(8,128)(2,1)}) custom-call(s32[1]{0:T(128)} %bitcast.1.me_ref, bf16[384,4096]{1,0:T(8,128)(2,1)} %gate_ref.1, bf16[384,4096]{1,0:T(8,128)(2,1)} %up_ref.1, bf16[1024,1536]{1,0:T(8,128)(2,1)} %down_ref.1), custom_call_target="tpu_custom_call" | custom-call | tf_op jit(solution)/shard_map/ffn_slices/pallas_call | solution.py:427
  45.0 5.0 collective-permute-start.22
  65.7 10.5 %collective-permute-start.20 = (bf16[48,1536]{1,0:T(8,128)(2,1)}, bf16[48,1536]{1,0:T(8,128)(2,1)S(1)}, u32[]{:S(2)}, u32[]{:S(2)}) collective-permute-start(bf16[48,1536]{1,0:T(8,128)(2,1)} %constant_dynamic-slice_fusion.36), channel_id=1, source_target_pairs={{0,1},{1,0},{2,3},{3,2},{4,5},{5,4},{6,7},{7,6},{8,9},{9,8},{10,11... | collective-permute-start | bytes 442376 | tf_op jit(solution)/shard_map/ppermute | solution.py:52
  81.8 6.5 %collective-permute-done.20 = bf16[48,1536]{1,0:T(8,128)(2,1)S(1)} collective-permute-done((bf16[48,1536]{1,0:T(8,128)(2,1)}, bf16[48,1536]{1,0:T(8,128)(2,1)S(1)}, u32[]{:S(2)}, u32[]{:S(2)}) %collective-permute-start.20) | collective-permute-done | bytes 147488 | tf_op jit(solution)/shard_map/ppermute | solution.py:52
  91.7 6.7 %collective-permute-done.12 = bf16[384,384]{1,0:T(8,128)(2,1)S(1)} collective-permute-done((bf16[384,384]{1,0:T(8,128)(2,1)}, bf16[384,384]{1,0:T(8,128)(2,1)S(1)}, u32[]{:S(2)}, u32[]{:S(2)}) %collective-permute-start.12) | collective-permute-done | bytes 294944 | tf_op jit(solution)/shard_map/ppermute | solution.py:52
  100.0 13.5 %collective-permute-done.11 = bf16[384,384]{1,0:T(8,128)(2,1)S(1)} collective-permute-done((bf16[384,384]{1,0:T(8,128)(2,1)}, bf16[384,384]{1,0:T(8,128)(2,1)S(1)}, u32[]{:S(2)}, u32[]{:S(2)}) %collective-permute-start.11) | collective-permute-done | bytes 294944 | tf_op jit(solution)/shard_map/ppermute | solution.py:52
  119.5 6.9 %collective-permute-done.8.refs_6_ = bf16[128,1536]{1,0:T(8,128)(2,1)S(1)} collective-permute-done((bf16[128,1536]{1,0:T(8,128)(2,1)S(1)}, bf16[128,1536]{1,0:T(8,128)(2,1)S(1)}, u32[]{:S(2)}, u32[]{:S(2)}) %collective-permute-start.8) | collective-permute-done | bytes 393248 | tf_op jit(solution)/shard_map/ppermute | solution.py:52
  129.6 7.2 %collective-permute-done.24 = bf16[4,48,1536]{2,1,0:T(8,128)(2,1)S(1)} collective-permute-done((bf16[4,48,1536]{2,1,0:T(8,128)(2,1)S(1)}, bf16[4,48,1536]{2,1,0:T(8,128)(2,1)S(1)}, u32[]{:S(2)}, u32[]{:S(2)}) %collective-permute-start.24) | collective-permute-done | bytes 589856 | tf_op jit(solution)/shard_map/ppermute | solution.py:52
  140.0 10.9 %attention_forward.1 = (bf16[1024,1536]{1,0:T(8,128)(2,1)}, bf16[1024,512]{1,0:T(8,128)(2,1)}, f32[1024,256]{1,0:T(8,128)}, f32[1024,128]{1,0:T(8,128)}, bf16[12...) custom-call(s32[2]{0:T(128)} %pad_add_fusion.info_ref, ...), custom_call_target="tpu_custom_call" | custom-call | tf_op jit(solution)/shard_map/attention_forward/pallas_call | solution.py:200
  174.8 8.5 %collective-permute-done.31.refs_2_ = bf16[128,1536]{1,0:T(8,128)(2,1)S(1)} collective-permute-done((bf16[128,1536]{1,0:T(8,128)(2,1)S(1)}, bf16[128,1536]{1,0:T(8,128)(2,1)S(1)}, u32[]{:S(2)}, u32[]{:S(2)}) %collective-permute-start.31) | collective-permute-done | bytes 393248 | tf_op jit(solution)/shard_map/ppermute | solution.py:52
  183.3 6.8 %collective-permute-done.33.refs_4_ = bf16[128,1536]{1,0:T(8,128)(2,1)S(1)} collective-permute-done((bf16[128,1536]{1,0:T(8,128)(2,1)S(1)}, bf16[128,1536]{1,0:T(8,128)(2,1)S(1)}, u32[]{:S(2)}, u32[]{:S(2)}) %collective-permute-start.33) | collective-permute-done | bytes 393248 | tf_op jit(solution)/shard_map/ppermute | solution.py:52
  193.7 11.2 %ffn_forward.1 = (bf16[1024,1536]{1,0:T(8,128)(2,1)}, bf16[1024,512]{1,0:T(8,128)(2,1)}, bf16[1024,1024]{1,0:T(8,128)(2,1)}, bf16[128,1536]{1,0:T(8,128)(2,1)}, ...) custom-call(bf16[128,1536]{1,0:T(8,128)(2,1)} %copy-done.17, ...), custom_call_target="tpu_custom_call" | custom-call | tf_op jit(solution)/shard_map/ffn_forward/pallas_call | solution.py:347
  224.4 7.1 %collective-permute-done.41 = bf16[128,1536]{1,0:T(8,128)(2,1)} collective-permute-done((bf16[128,1536]{1,0:T(8,128)(2,1)}, bf16[128,1536]{1,0:T(8,128)(2,1)}, u32[]{:S(2)}, u32[]{:S(2)}) %collective-permute-start.41) | collective-permute-done | bytes 393248 | tf_op jit(solution)/shard_map/ppermute | solution.py:52
  237.5 8.6 %collective-permute-done.52.refs_2_ = bf16[128,1536]{1,0:T(8,128)(2,1)S(1)} collective-permute-done((bf16[128,1536]{1,0:T(8,128)(2,1)S(1)}, bf16[128,1536]{1,0:T(8,128)(2,1)S(1)}, u32[]{:S(2)}, u32[]{:S(2)}) %collective-permute-start.52) | collective-permute-done | bytes 393248 | tf_op jit(solution)/shard_map/ppermute | solution.py:52
  246.1 5.7 collective-permute-done.54.refs_4_
  256.0 22.3 %ffn_backward.1 = (bf16[1024,1536]{1,0:T(8,128)(2,1)}, bf16[1024,1024]{1,0:T(8,128)(2,1)}, bf16[128,1536]{1,0:T(8,128)(2,1)}, bf16[128,1536]{1,0:T(8,128)(2,1)},...) custom-call(bf16[128,1536]{1,0:T(8,128)(2,1)} %copy-done.15, ...), custom_call_target="tpu_custom_call" | custom-call | tf_op jit(solution)/shard_map/ffn_backward/pallas_call | solution.py:389
  278.4 4.9 convolution_convert_fusion.2
  291.4 6.5 %convolution_convert_fusion.1 = bf16[1536,1024]{1,0:T(8,128)(2,1)} fusion(bf16[1024,1536]{1,0:T(8,128)(2,1)S(1)} %copy-done.92, bf16[1024,1024]{1,0:T(8,128)(2,1)} %get-tuple-element.100), kind=kOutput, calls=%fused_computation.1 | convolution fusion | flops 3222798336 | bytes 8388608 | tf_op jit(solution)/shard_map/dot_general | solution.py:37
  299.9 8.8 %collective-permute-done.62 = bf16[128,1536]{1,0:T(8,128)(2,1)} collective-permute-done((bf16[128,1536]{1,0:T(8,128)(2,1)S(1)}, bf16[128,1536]{1,0:T(8,128)(2,1)}, u32[]{:S(2)}, u32[]{:S(2)}) %collective-permute-start.62) | collective-permute-done | bytes 393248 | tf_op jit(solution)/shard_map/ppermute | solution.py:52
  340.2 4.3 collective-permute-start.48
  350.2 11.5 %attention_backward.1 = (bf16[1024,384]{1,0:T(8,128)(2,1)}, bf16[128,1536]{1,0:T(8,128)(2,1)}, bf16[128,1536]{1,0:T(8,128)(2,1)}, bf16[128,1536]{1,0:T(8,128)(2,...) custom-call(s32[2]{0:T(128)} %pad_add_fusion.info_ref, ...), custom_call_target="tpu_custom_call" | custom-call | tf_op jit(solution)/shard_map/attention_backward/pallas_call | solution.py:299
  375.2 9.6 %collective-permute-done.81 = bf16[384,384]{0,1:T(8,128)(2,1)} collective-permute-done((bf16[384,384]{0,1:T(8,128)(2,1)}, bf16[384,384]{0,1:T(8,128)(2,1)}, u32[]{:S(2)}, u32[]{:S(2)}) %collective-permute-start.81) | collective-permute-done | bytes 294944 | tf_op jit(solution)/shard_map/ppermute | solution.py:52
  384.8 20.8 %collective-permute-done.80 = bf16[384,384]{0,1:T(8,128)(2,1)} collective-permute-done((bf16[384,384]{0,1:T(8,128)(2,1)}, bf16[384,384]{0,1:T(8,128)(2,1)}, u32[]{:S(2)}, u32[]{:S(2)}) %collective-permute-start.80) | collective-permute-done | bytes 294944 | tf_op jit(solution)/shard_map/ppermute | solution.py:52
  422.0 6.8 %collective-permute-done.78 = bf16[128,1536]{1,0:T(8,128)(2,1)S(1)} collective-permute-done((bf16[128,1536]{1,0:T(8,128)(2,1)S(1)}, bf16[128,1536]{1,0:T(8,128)(2,1)S(1)}, u32[]{:S(2)}, u32[]{:S(2)}) %collective-permute-start.78) | collective-permute-done | bytes 393248 | tf_op jit(solution)/shard_map/ppermute | solution.py:52
  428.8 8.6 %collective-permute-done.74 = bf16[128,1536]{1,0:T(8,128)(2,1)S(1)} collective-permute-done((bf16[128,1536]{1,0:T(8,128)(2,1)S(1)}, bf16[128,1536]{1,0:T(8,128)(2,1)S(1)}, u32[]{:S(2)}, u32[]{:S(2)}) %collective-permute-start.74) | collective-permute-done | bytes 393248 | tf_op jit(solution)/shard_map/ppermute | solution.py:52
  460.2 4.9 collective-permute-done.87
  479.7 10.0 %collective-permute-done.91 = bf16[192,1536]{1,0:T(8,128)(2,1)} collective-permute-done((bf16[192,1536]{1,0:T(8,128)(2,1)}, bf16[192,1536]{1,0:T(8,128)(2,1)}, u32[]{:S(2)}, u32[]{:S(2)}) %collective-permute-start.91) | collective-permute-done | bytes 589856 | tf_op jit(solution)/shard_map/ppermute | solution.py:52
  500.3 5.3 collective-permute-done.97
  514.1 6.4 %collective-permute-done.102 = bf16[48,1536]{1,0:T(8,128)(2,1)S(1)} collective-permute-done((bf16[48,1536]{1,0:T(8,128)(2,1)}, bf16[48,1536]{1,0:T(8,128)(2,1)S(1)}, u32[]{:S(2)}, u32[]{:S(2)}) %collective-permute-start.102) | collective-permute-done | bytes 147488 | tf_op jit(solution)/shard_map/ppermute | solution.py:52
  526.9 7.5 %collective-permute-done.114.refs_10_ = bf16[128,1536]{1,0:T(8,128)(2,1)S(1)} collective-permute-done((bf16[128,1536]{1,0:T(8,128)(2,1)}, bf16[128,1536]{1,0:T(8,128)(2,1)S(1)}, u32[]{:S(2)}, u32[]{:S(2)}) %collective-permute-start.114) | collective-permute-done | bytes 393248 | tf_op jit(solution)/shard_map/ppermute | solution.py:52
  535.0 41.0 %collective-permute-done.118.refs_14_ = bf16[128,1536]{1,0:T(8,128)(2,1)S(1)} collective-permute-done((bf16[128,1536]{1,0:T(8,128)(2,1)}, bf16[128,1536]{1,0:T(8,128)(2,1)S(1)}, u32[]{:S(2)}, u32[]{:S(2)}) %collective-permute-start.118) | collective-permute-done | bytes 393248 | tf_op jit(solution)/shard_map/ppermute | solution.py:52
  585.4 10.5 %ffn_grads.1 = (f32[384,4096]{1,0:T(8,128)}, f32[384,4096]{1,0:T(8,128)}, f32[1024,1536]{1,0:T(8,128)}) custom-call(s32[1]{0:T(128)} %bitcast.1.me_ref, bf16[384,1024]{1,0:T(8,128)(2,1)} %reduce-scatter.3.cloned.1.call-done.refs_0_, bf16[384,1024]{1,0:T(8,128)(2,1)} %copy-done.34, bf16[384,1024]{1,0:T(8,128)(2,1)} %copy-done.31, ...), custom_call_target="tpu_custom_call" | custom-call | tf_op jit(solution)/shard_map/ffn_grads/pallas_call | solution.py:487
  (613 shorter events, 239.3 us)
Async XLA Ops:
  7.2 186.5 %all-gather.5.cloned.1.call-start = ((), (), s32[]{:S(2)}) async-start(), calls=%async_computation.3 | async-start | bytes 1966080 | tf_op jit(solution)/shard_map/all_gather | solution.py:549
  44.2 149.4 %all-gather.3.cloned.1.call-start = ((), (), s32[]{:S(2)}) async-start(), calls=%async_computation.2 | async-start | bytes 3932160 | tf_op jit(solution)/shard_map/all_gather | solution.py:548
  45.0 36.1 %collective-permute-start.22 = (bf16[48,1536]{1,0:T(8,128)(2,1)}, bf16[48,1536]{1,0:T(8,128)(2,1)}, u32[]{:S(2)}, u32[]{:S(2)}) collective-permute-start(bf16[48,1536]{1,0:T(8,128)(2,1)} %constant_dynamic-slice_fusion.36), channel_id=1, source_target_pairs={{0,3},{1,2},{2,1},{3,0},{4,7},{5,6},{6,5},{7,4},{8,11},{9,10},{10,... | collective-permute-start | bytes 442376 | tf_op jit(solution)/shard_map/ppermute | solution.py:52
  50.0 31.8 %collective-permute-start.21 = (bf16[48,1536]{1,0:T(8,128)(2,1)}, bf16[48,1536]{1,0:T(8,128)(2,1)}, u32[]{:S(2)}, u32[]{:S(2)}) collective-permute-start(bf16[48,1536]{1,0:T(8,128)(2,1)} %constant_dynamic-slice_fusion.36), channel_id=1, source_target_pairs={{0,2},{1,3},{2,0},{3,1},{4,6},{5,7},{6,4},{7,5},{8,10},{9,11},{10,... | collective-permute-start | bytes 442376 | tf_op jit(solution)/shard_map/ppermute | solution.py:52
  53.5 26.5 %collective-permute-start = (bf16[2,384]{1,0:T(2,128)(2,1)}, bf16[2,384]{1,0:T(2,128)(2,1)}, u32[]{:S(2)}, u32[]{:S(2)}) collective-permute-start(bf16[2,384]{1,0:T(2,128)(2,1)} %pad_maximum_fusion.12), channel_id=1, source_target_pairs={{0,1},{1,0},{2,3},{3,2},{4,5},{5,4},{6,7},{7,6},{8,9},{9,8},{10,11... | collective-permute-start | bytes 4616 | tf_op jit(solution)/shard_map/ppermute | solution.py:52
  55.0 466.9 %reduce-scatter.5.cloned.1.call-start = ((), (), s32[]{:S(2)}) async-start(), calls=%async_computation.5 | async-start | bytes 1966080 | tf_op jit(solution)/shard_map/reduce_scatter | solution.py:605
  80.1 33.4 %collective-permute-start.11 = (bf16[384,384]{1,0:T(8,128)(2,1)}, bf16[384,384]{1,0:T(8,128)(2,1)S(1)}, u32[]{:S(2)}, u32[]{:S(2)}) collective-permute-start(bf16[384,384]{1,0:T(8,128)(2,1)} %pad_maximum_fusion.7), channel_id=1, source_target_pairs={{0,2},{1,3},{2,0},{3,1},{4,6},{5,7},{6,4},{7,5},{8,10},{9,11},{10,... | collective-permute-start | bytes 884744 | tf_op jit(solution)/shard_map/ppermute | solution.py:52
  81.1 34.8 %collective-permute-start.10 = (bf16[384,384]{1,0:T(8,128)(2,1)}, bf16[384,384]{1,0:T(8,128)(2,1)}, u32[]{:S(2)}, u32[]{:S(2)}) collective-permute-start(bf16[384,384]{1,0:T(8,128)(2,1)} %pad_maximum_fusion.7), channel_id=1, source_target_pairs={{0,1},{1,0},{2,3},{3,2},{4,5},{5,4},{6,7},{7,6},{8,9},{9,8},{10,11... | collective-permute-start | bytes 884744 | tf_op jit(solution)/shard_map/ppermute | solution.py:52
  89.5 36.9 %collective-permute-start.23 = (bf16[4,48,1536]{2,1,0:T(8,128)(2,1)S(1)}, bf16[4,48,1536]{2,1,0:T(8,128)(2,1)}, u32[]{:S(2)}, u32[]{:S(2)}) collective-permute-start(bf16[4,48,1536]{2,1,0:T(8,128)(2,1)S(1)} %pad_maximum_fusion.3), channel_id=1, source_target_pairs={{0,4},{4,0},{8,12},{12,8},{16,20},{20,16},{24,28},{28,24},{1,5},{5... | collective-permute-start | bytes 1769480 | tf_op jit(solution)/shard_map/ppermute | solution.py:52
  90.2 28.7 %collective-permute-start.4 = (bf16[128,1536]{1,0:T(8,128)(2,1)S(1)}, bf16[128,1536]{1,0:T(8,128)(2,1)}, u32[]{:S(2)}, u32[]{:S(2)}) collective-permute-start(bf16[128,1536]{1,0:T(8,128)(2,1)S(1)} %pad_maximum_fusion.4.refs_0_), channel_id=1, source_target_pairs={{0,8},{4,12},{8,0},{12,4},{16,24},{20,28},{24,16},{28,20},{1,9},{5... | collective-permute-start | bytes 1179656 | tf_op jit(solution)/shard_map/ppermute | solution.py:52
  128.0 30.0 %collective-permute-start.26 = (bf16[4,48,1536]{2,1,0:T(8,128)(2,1)S(1)}, bf16[4,48,1536]{2,1,0:T(8,128)(2,1)}, u32[]{:S(2)}, u32[]{:S(2)}) collective-permute-start(bf16[4,48,1536]{2,1,0:T(8,128)(2,1)S(1)} %pad_maximum_fusion.3), channel_id=1, source_target_pairs={{0,16},{4,20},{8,24},{12,28},{16,0},{20,4},{24,8},{28,12},{1,17},{... | collective-permute-start | bytes 1769480 | tf_op jit(solution)/shard_map/ppermute | solution.py:52
  136.8 24.3 %collective-permute-start.28 = (bf16[4,48,1536]{2,1,0:T(8,128)(2,1)S(1)}, bf16[4,48,1536]{2,1,0:T(8,128)(2,1)}, u32[]{:S(2)}, u32[]{:S(2)}) collective-permute-start(bf16[4,48,1536]{2,1,0:T(8,128)(2,1)S(1)} %pad_maximum_fusion.3), channel_id=1, source_target_pairs={{0,24},{4,28},{8,16},{12,20},{16,8},{20,12},{24,0},{28,4},{1,25},{... | collective-permute-start | bytes 1769480 | tf_op jit(solution)/shard_map/ppermute | solution.py:52
  138.3 25.5 %collective-permute-start.25 = (bf16[4,48,1536]{2,1,0:T(8,128)(2,1)S(1)}, bf16[4,48,1536]{2,1,0:T(8,128)(2,1)}, u32[]{:S(2)}, u32[]{:S(2)}) collective-permute-start(bf16[4,48,1536]{2,1,0:T(8,128)(2,1)S(1)} %collective-permute-done.24), channel_id=1, source_target_pairs={{0,4},{4,0},{8,12},{12,8},{16,20},{20,16},{24,28},{28,24},{1,5},{5... | collective-permute-start | bytes 1769480 | tf_op jit(solution)/shard_map/ppermute | solution.py:52
  283.4 240.0 %reduce-scatter.3.cloned.1.call-start = ((), (), s32[]{:S(2)}) async-start(), calls=%async_computation.4 | async-start | bytes 3932160 | tf_op jit(solution)/shard_map/reduce_scatter | solution.py:606
  320.5 24.6 %collective-permute-start.65 = (bf16[128,192]{1,0:T(8,128)(2,1)S(1)}, bf16[128,192]{1,0:T(8,128)(2,1)S(1)}, u32[]{:S(2)}, u32[]{:S(2)}) collective-permute-start(bf16[128,192]{1,0:T(8,128)(2,1)S(1)} %get-tuple-element.193), channel_id=1, source_target_pairs={{0,4},{4,0},{8,12},{12,8},{16,20},{20,16},{24,28},{28,24},{1,5},{5... | collective-permute-start | bytes 147464 | tf_op jit(solution)/shard_map/ppermute | solution.py:52
  340.2 27.4 %collective-permute-start.48 = (f32[1]{0:T(128)}, f32[1]{0:T(128)}, u32[]{:S(2)}, u32[]{:S(2)}) collective-permute-start(f32[1]{0:T(128)} %add.369), channel_id=1, source_target_pairs={{0,2},{1,3},{2,0},{3,1},{4,6},{5,7},{6,4},{7,5},{8,10},{9,11},{10,... | collective-permute-start | bytes 20 | tf_op jit(solution)/shard_map/ppermute | solution.py:52
  346.4 27.0 %collective-permute-start.130 = (f32[384]{0:T(512)}, f32[384]{0:T(512)}, u32[]{:S(2)}, u32[]{:S(2)}) collective-permute-start(f32[384]{0:T(512)} %get-tuple-element.112), channel_id=1, source_target_pairs={{0,2},{1,3},{2,0},{3,1},{4,6},{5,7},{6,4},{7,5},{8,10},{9,11},{10,... | collective-permute-start | bytes 4616 | tf_op jit(solution)/shard_map/ppermute | solution.py:52
  346.8 26.7 %collective-permute-start.129 = (f32[384]{0:T(512)}, f32[384]{0:T(512)}, u32[]{:S(2)}, u32[]{:S(2)}) collective-permute-start(f32[384]{0:T(512)} %get-tuple-element.110), channel_id=1, source_target_pairs={{0,1},{1,0},{2,3},{3,2},{4,5},{5,4},{6,7},{7,6},{8,9},{9,8},{10,11... | collective-permute-start | bytes 4616 | tf_op jit(solution)/shard_map/ppermute | solution.py:52
  367.6 38.1 %collective-permute-start.80 = (bf16[384,384]{0,1:T(8,128)(2,1)}, bf16[384,384]{0,1:T(8,128)(2,1)}, u32[]{:S(2)}, u32[]{:S(2)}) collective-permute-start(bf16[384,384]{0,1:T(8,128)(2,1)} %get-tuple-element.147), channel_id=1, source_target_pairs={{0,2},{1,3},{2,0},{3,1},{4,6},{5,7},{6,4},{7,5},{8,10},{9,11},{10,... | collective-permute-start | bytes 884744 | tf_op jit(solution)/shard_map/ppermute | solution.py:52
  367.8 37.9 %collective-permute-start.79 = (bf16[384,384]{0,1:T(8,128)(2,1)}, bf16[384,384]{0,1:T(8,128)(2,1)}, u32[]{:S(2)}, u32[]{:S(2)}) collective-permute-start(bf16[384,384]{0,1:T(8,128)(2,1)} %get-tuple-element.145), channel_id=1, source_target_pairs={{0,1},{1,0},{2,3},{3,2},{4,5},{5,4},{6,7},{7,6},{8,9},{9,8},{10,11... | collective-permute-start | bytes 884744 | tf_op jit(solution)/shard_map/ppermute | solution.py:52
  373.4 38.5 %collective-permute-start.94 = (bf16[192,1536]{1,0:T(8,128)(2,1)}, bf16[192,1536]{1,0:T(8,128)(2,1)S(1)}, u32[]{:S(2)}, u32[]{:S(2)}) collective-permute-start(bf16[192,1536]{1,0:T(8,128)(2,1)} %bitcast.257), channel_id=1, source_target_pairs={{0,4},{4,0},{8,12},{12,8},{16,20},{20,16},{24,28},{28,24},{1,5},{5... | collective-permute-start | bytes 1769480 | tf_op jit(solution)/shard_map/ppermute | solution.py:52
  373.5 34.9 %collective-permute-start.77 = (bf16[128,1536]{1,0:T(8,128)(2,1)}, bf16[128,1536]{1,0:T(8,128)(2,1)S(1)}, u32[]{:S(2)}, u32[]{:S(2)}) collective-permute-start(bf16[128,1536]{1,0:T(8,128)(2,1)} %get-tuple-element.96), channel_id=1, source_target_pairs={{0,4},{4,0},{8,12},{12,8},{16,20},{20,16},{24,28},{28,24},{1,5},{5... | collective-permute-start | bytes 1179656 | tf_op jit(solution)/shard_map/ppermute | solution.py:52
  384.8 28.7 %collective-permute-start.92 = (bf16[192,1536]{1,0:T(8,128)(2,1)}, bf16[192,1536]{1,0:T(8,128)(2,1)S(1)}, u32[]{:S(2)}, u32[]{:S(2)}) collective-permute-start(bf16[192,1536]{1,0:T(8,128)(2,1)} %bitcast.256), channel_id=1, source_target_pairs={{0,4},{4,0},{8,12},{12,8},{16,20},{20,16},{24,28},{28,24},{1,5},{5... | collective-permute-start | bytes 1769480 | tf_op jit(solution)/shard_map/ppermute | solution.py:52
  420.5 36.2 %collective-permute-start.85 = (bf16[384,384]{0,1:T(8,128)(2,1)}, bf16[384,384]{0,1:T(8,128)(2,1)}, u32[]{:S(2)}, u32[]{:S(2)}) collective-permute-start(bf16[384,384]{0,1:T(8,128)(2,1)} %get-tuple-element.123), channel_id=1, source_target_pairs={{0,16},{4,20},{8,24},{12,28},{16,0},{20,4},{24,8},{28,12},{1,17},{... | collective-permute-start | bytes 884744 | tf_op jit(solution)/shard_map/ppermute | solution.py:52
  428.8 29.3 %collective-permute-start.84 = (bf16[384,384]{0,1:T(8,128)(2,1)}, bf16[384,384]{0,1:T(8,128)(2,1)}, u32[]{:S(2)}, u32[]{:S(2)}) collective-permute-start(bf16[384,384]{0,1:T(8,128)(2,1)} %collective-permute-done.83), channel_id=1, source_target_pairs={{0,4},{4,0},{8,12},{12,8},{16,20},{20,16},{24,28},{28,24},{1,5},{5... | collective-permute-start | bytes 884744 | tf_op jit(solution)/shard_map/ppermute | solution.py:52
  453.7 25.9 %collective-permute-start.89 = (bf16[192,1536]{1,0:T(8,128)(2,1)}, bf16[192,1536]{1,0:T(8,128)(2,1)}, u32[]{:S(2)}, u32[]{:S(2)}) collective-permute-start(bf16[192,1536]{1,0:T(8,128)(2,1)} %bitcast.69), channel_id=1, source_target_pairs={{0,4},{4,0},{8,12},{12,8},{16,20},{20,16},{24,28},{28,24},{1,5},{5... | collective-permute-start | bytes 1769480 | tf_op jit(solution)/shard_map/ppermute | solution.py:52
  465.1 24.6 %collective-permute-start.91 = (bf16[192,1536]{1,0:T(8,128)(2,1)}, bf16[192,1536]{1,0:T(8,128)(2,1)}, u32[]{:S(2)}, u32[]{:S(2)}) collective-permute-start(bf16[192,1536]{1,0:T(8,128)(2,1)} %fusion.2), channel_id=1, source_target_pairs={{0,24},{4,28},{8,16},{12,20},{16,8},{20,12},{24,0},{28,4},{1,25},{... | collective-permute-start | bytes 1769480 | tf_op jit(solution)/shard_map/ppermute | solution.py:52
  523.3 53.2 %collective-permute-start.107 = (bf16[384,1024]{1,0:T(8,128)(2,1)}, bf16[384,1024]{1,0:T(8,128)(2,1)S(1)}, u32[]{:S(2)}, u32[]{:S(2)}) collective-permute-start(bf16[384,1024]{1,0:T(8,128)(2,1)} %reduce-scatter.3.cloned.1.call-done.refs_0_), channel_id=1, source_target_pairs={{0,8},{4,12},{8,0},{12,4},{16,24},{20,28},{24,16},{28,20},{1,9},{5... | collective-permute-start | bytes 2359304 | tf_op jit(solution)/shard_map/ppermute | solution.py:52
  524.8 51.8 %collective-permute-start.109 = (bf16[384,1024]{1,0:T(8,128)(2,1)}, bf16[384,1024]{1,0:T(8,128)(2,1)S(1)}, u32[]{:S(2)}, u32[]{:S(2)}) collective-permute-start(bf16[384,1024]{1,0:T(8,128)(2,1)} %reduce-scatter.3.cloned.1.call-done.refs_0_), channel_id=1, source_target_pairs={{0,16},{4,20},{8,24},{12,28},{16,0},{20,4},{24,8},{28,12},{1,17},{... | collective-permute-start | bytes 2359304 | tf_op jit(solution)/shard_map/ppermute | solution.py:52
  526.3 50.8 %collective-permute-start.111 = (bf16[384,1024]{1,0:T(8,128)(2,1)}, bf16[384,1024]{1,0:T(8,128)(2,1)S(1)}, u32[]{:S(2)}, u32[]{:S(2)}) collective-permute-start(bf16[384,1024]{1,0:T(8,128)(2,1)} %reduce-scatter.3.cloned.1.call-done.refs_0_), channel_id=1, source_target_pairs={{0,24},{4,28},{8,16},{12,20},{16,8},{20,12},{24,0},{28,4},{1,25},{... | collective-permute-start | bytes 2359304 | tf_op jit(solution)/shard_map/ppermute | solution.py:52
  534.4 41.7 %collective-permute-start.118 = (bf16[128,1536]{1,0:T(8,128)(2,1)}, bf16[128,1536]{1,0:T(8,128)(2,1)S(1)}, u32[]{:S(2)}, u32[]{:S(2)}) collective-permute-start(bf16[128,1536]{1,0:T(8,128)(2,1)} %reduce-scatter.5.cloned.1.call-done.refs_8_), channel_id=1, source_target_pairs={{0,24},{4,28},{8,16},{12,20},{16,8},{20,12},{24,0},{28,4},{1,25},{... | collective-permute-start | bytes 1179656 | tf_op jit(solution)/shard_map/ppermute | solution.py:52
  535.0 41.1 %collective-permute-start.115 = (bf16[128,1536]{1,0:T(8,128)(2,1)S(1)}, bf16[128,1536]{1,0:T(8,128)(2,1)}, u32[]{:S(2)}, u32[]{:S(2)}) collective-permute-start(bf16[128,1536]{1,0:T(8,128)(2,1)S(1)} %collective-permute-done.114.refs_10_), channel_id=1, source_target_pairs={{0,4},{4,0},{8,12},{12,8},{16,20},{20,16},{24,28},{28,24},{1,5},{5... | collective-permute-start | bytes 1179656 | tf_op jit(solution)/shard_map/ppermute | solution.py:52
  (199 other events, 2217.3 us)
Sparse Core Ops, SparseCore 0:
  44.4 63.6 all-gather.4
  110.2 63.8 all-gather.2
  283.5 35.3 reduce-scatter.4
  321.6 69.1 reduce-scatter.2
